TPU v7x, 256 devices: a whole 4x4x8 slice. The times are simulated.
256 devices in a mesh: dp: 16 (over x_lo, z), ctx: 16 (over y, x_hi, core).
Axes of the slice: x: 4 (x_hi: 2, x_lo: 2; x = x_hi * 2 + x_lo), y: 4, z: 8, core: 2. Of those that a mesh axis runs over, the one named last changes fastest.
Arguments:
- hidden: bfloat16 [16, 2048, 4096], P('dp', 'ctx'), may hold values from -6 to 6
- value_weight: bfloat16 [4096, 512], P(('dp', 'ctx')), may hold values from -0.09375 to 0.09375
- queries: bfloat16 [16, 2048, 4096], P('dp', 'ctx'), may hold values from -4.5 to 4.5
- key_rows: bfloat16 [16, 2048, 512], P('dp', 'ctx'), may hold values from -4.5 to 4.5
- attn_saved: bfloat16 [16, 2048, 4096], P('dp', 'ctx'), may hold values from -3 to 3
- grad_out: bfloat16 [16, 2048, 4096], P('dp', 'ctx'), may hold values from -6 to 6
- doc_lengths: int32 [16, 8], P('dp'), may hold values from 1 to 1024, 2048 in all within a row
- routing: int32 [16, 2048], P('dp'), may hold values from 0 to 2047, as said below
- visible_blocks: int32 [16, 32, 32], P('dp'), may hold values from 0 to 1, as said below
Outputs:
- grad_query: bfloat16 [16, 2048, 4096], P('dp', 'ctx')
- grad_key: bfloat16 [16, 2048, 512], P('dp', 'ctx')
- grad_value_weight: float32 [4096, 512], P(('dp', 'ctx'))
Inputs may be any that keep to these rules, and one draw needn't show every extreme that they name: For each pack, routing is a permutation: the token at position i, held by device i // 128 of ctx, goes to owner slot routing[i], held by device routing[i] // 128 of ctx, so every owner device receives 128 tokens. At most 16 tokens of one device go to one owner device, and this bound is reached in every draw. visible_blocks[b, b] = 1 for every block b. `doc_lengths`: each pack's lengths sum to 2048; the longest is 1024.
All inputs are finite; a program needn't handle non-finite values.
Results may differ from a plain program's by a relative error of at most 0.023.
Values may be sent and summed in bfloat16 or wider, within the bound.
A program may use at most 128 MiB of HBM per device.

v0:
```python
import math

import jax
import jax.numpy as jnp
from jax import lax
from jax.sharding import PartitionSpec as P

QH = 32
KVH = 4
HD = 128
VB = 64


far_below = -1e30


def document_index(positions, doc_lengths):
    doc_ends = jnp.cumsum(doc_lengths)
    return jnp.sum((positions[:, None] >= doc_ends[None, :]).astype(jnp.int32), axis=1)


def merge_pairs(first, second):
    top = jnp.maximum(first[0], second[0])
    return (top, first[1] * jnp.exp(first[0] - top) + second[1] * jnp.exp(second[0] - top))


def local(
    hidden,
    value_weight,
    queries,
    key_rows,
    attn_saved,
    grad_out,
    doc_lengths,
    routing,
    visible_blocks,
):
    row_count = hidden.shape[1]
    ctx_count = lax.axis_size("ctx")
    dp_count = lax.axis_size("dp")
    ctx_place = lax.axis_index("ctx")
    token_count = routing.shape[1]
    capacity = 2 * row_count // ctx_count
    slot_count = ctx_count * capacity
    group_size = QH // KVH
    kv_width = key_rows.shape[2]
    score_scale = 1.0 / math.sqrt(HD)
    features = hidden[0]
    slot_route = routing[0]
    lengths = doc_lengths[0]
    block_table = visible_blocks[0].astype(jnp.float32)
    block_count = block_table.shape[0]
    columns = features
    projected = jnp.dot(
        columns,
        lax.all_gather(value_weight, ("dp", "ctx"), axis=0, tiled=True),
        preferred_element_type=jnp.float32,
    )
    value_rows = projected.astype(jnp.bfloat16)
    token_iota = jnp.arange(token_count, dtype=jnp.int32)
    slot_position = jnp.zeros((token_count,), jnp.int32).at[slot_route].set(token_iota)
    query_position = lax.dynamic_slice_in_dim(slot_position, ctx_place * row_count, row_count)
    local_route = lax.dynamic_slice_in_dim(slot_route, ctx_place * row_count, row_count)
    device_iota = jnp.arange(ctx_count, dtype=jnp.int32)
    target = local_route // row_count
    matches = (target[:, None] == device_iota[None, :]).astype(jnp.int32)
    earlier = jnp.cumsum(matches, axis=0) - matches
    send_slot = target * capacity + jnp.sum(earlier * matches, axis=1)
    buffer_iota = jnp.arange(slot_count, dtype=jnp.int32)
    send_matrix = (buffer_iota[:, None] == send_slot[None, :]).astype(jnp.bfloat16)
    owner_table = slot_route.reshape(ctx_count, row_count) // row_count
    coming = (owner_table == ctx_place).astype(jnp.int32)
    arrival = (device_iota[:, None] * capacity + jnp.cumsum(coming, axis=1) - coming).reshape(
        token_count
    )
    arrive_slot = arrival[query_position]
    receive_matrix = (arrive_slot[:, None] == buffer_iota[None, :]).astype(jnp.bfloat16)

    def to_slots(source_rows):
        placed = jnp.dot(send_matrix, source_rows, preferred_element_type=jnp.float32).astype(
            jnp.bfloat16
        )
        return placed.reshape(ctx_count, capacity, source_rows.shape[1])

    def from_slots(arrived):
        flat_rows = arrived.reshape(slot_count, arrived.shape[2])
        return jnp.dot(receive_matrix, flat_rows, preferred_element_type=jnp.float32).astype(
            jnp.bfloat16
        )

    local_pair = jnp.concatenate([key_rows[0], value_rows], axis=1)
    got_query, got_grad, got_pair = (
        lax.all_to_all(to_slots(queries[0]), "ctx", split_axis=0, concat_axis=0, tiled=True),
        lax.all_to_all(to_slots(grad_out[0]), "ctx", split_axis=0, concat_axis=0, tiled=True),
        lax.all_to_all(to_slots(local_pair), "ctx", split_axis=0, concat_axis=0, tiled=True),
    )
    pair_rows = from_slots(got_pair)
    owner_query = from_slots(got_query)
    owner_grad = from_slots(got_grad)
    pair_whole = lax.all_gather(pair_rows, "ctx", axis=0, tiled=True)
    query_docs = document_index(query_position, lengths)
    key_docs = document_index(slot_position, lengths)
    block_iota = jnp.arange(block_count, dtype=jnp.int32)
    query_onehot = (query_position[:, None] // VB == block_iota[None, :]).astype(jnp.float32)
    row_visible = jnp.dot(query_onehot, block_table, preferred_element_type=jnp.float32)
    key_onehot = (slot_position[:, None] // VB == block_iota[None, :]).astype(jnp.float32)
    visible = jnp.dot(row_visible, key_onehot.T, preferred_element_type=jnp.float32)
    allowed = (
        (query_docs[:, None] == key_docs[None, :])
        & (slot_position[None, :] <= query_position[:, None])
        & (visible > 0.5)
    )
    presence = jnp.broadcast_to(
        allowed.astype(jnp.float32)[None], (group_size, row_count, token_count)
    )
    query_heads = owner_query.reshape(row_count, KVH, group_size, HD)
    grad_heads = owner_grad.reshape(row_count, KVH, group_size, HD)
    saved_heads = attn_saved[0].astype(jnp.float32).reshape(row_count, KVH, group_size, HD)
    row_delta = jnp.transpose(
        jnp.sum(grad_heads.astype(jnp.float32) * saved_heads, axis=-1), (1, 2, 0)
    )
    key_all = pair_whole[:, :kv_width].reshape(token_count, KVH, HD)
    value_all = pair_whole[:, kv_width:].reshape(token_count, KVH, HD)
    query_parts = []
    key_parts = []
    value_parts = []
    for kv_head in range(KVH):
        head_query = query_heads[:, kv_head]
        head_grad = grad_heads[:, kv_head]
        head_keys = key_all[:, kv_head]
        scores = (
            jnp.einsum("rjd,kd->jrk", head_query, head_keys, preferred_element_type=jnp.float32)
            * score_scale
        )
        masked = jnp.where(allowed[None], scores, far_below)
        row_top, row_total = lax.reduce(
            (masked, presence), (jnp.float32(far_below), jnp.float32(0.0)), merge_pairs, (2,)
        )
        log_total = (row_top + jnp.log(row_total))[..., None]
        weights = jnp.where(allowed[None], jnp.exp(scores - log_total), 0.0)
        weights_b = weights.astype(jnp.bfloat16)
        dweights = jnp.einsum(
            "rjd,kd->jrk", head_grad, value_all[:, kv_head], preferred_element_type=jnp.float32
        ).astype(jnp.bfloat16)
        dscores = (
            score_scale * weights * (dweights.astype(jnp.float32) - row_delta[kv_head][..., None])
        ).astype(jnp.bfloat16)
        query_parts.append(
            jnp.einsum("jrk,kd->rjd", dscores, head_keys, preferred_element_type=jnp.float32)
        )
        key_parts.append(
            jnp.einsum("jrk,rjd->kd", dscores, head_query, preferred_element_type=jnp.float32)
        )
        value_parts.append(
            jnp.einsum("jrk,rjd->kd", weights_b, head_grad, preferred_element_type=jnp.float32)
        )
    query_grad = jnp.stack(query_parts, axis=1)
    pair_terms = jnp.concatenate(
        [jnp.concatenate(key_parts, axis=1), jnp.concatenate(value_parts, axis=1)], axis=1
    )
    pair_sums = lax.psum_scatter(
        pair_terms.astype(jnp.bfloat16), "ctx", scatter_dimension=0, tiled=True
    )
    outgoing = jnp.dot(receive_matrix.T, pair_sums, preferred_element_type=jnp.float32).astype(
        jnp.bfloat16
    )
    returned = lax.all_to_all(
        outgoing.reshape(ctx_count, capacity, 2 * kv_width),
        "ctx",
        split_axis=0,
        concat_axis=0,
        tiled=True,
    )
    loader_grad = jnp.dot(
        send_matrix.T,
        returned.reshape(slot_count, 2 * kv_width),
        preferred_element_type=jnp.float32,
    ).astype(jnp.bfloat16)
    grad_value = loader_grad[:, kv_width:]
    weight_scale = 1.0 / math.sqrt(dp_count * token_count)
    columns = features
    weight_grad = lax.psum_scatter(
        jnp.einsum("rd,rk->dk", columns, grad_value, preferred_element_type=jnp.float32)
        * weight_scale,
        ("dp", "ctx"),
        scatter_dimension=0,
        tiled=True,
    )
    grad_query = query_grad.reshape(row_count, QH * HD).astype(jnp.bfloat16)
    return (grad_query[None], loader_grad[:, :kv_width][None], weight_grad)


def solution(mesh):
    placed = (
        P("dp", "ctx", None),
        P(("dp", "ctx"), None),
        P("dp", "ctx", None),
        P("dp", "ctx", None),
        P("dp", "ctx", None),
        P("dp", "ctx", None),
        P("dp", None),
        P("dp", None),
        P("dp", None, None),
    )
    return jax.shard_map(
        local,
        mesh=mesh,
        in_specs=placed,
        out_specs=(P("dp", "ctx", None), P("dp", "ctx", None), P(("dp", "ctx"), None)),
        check_vma=False,
    )
```

profile of v0, /device:TPU:128, one launch (start us, length us, event | category | flops | bytes accessed | tf_op | source)
XLA Modules:
  0.0 2083.1 jit_solution(7185739076317425619)
XLA Ops:
  8.6 8.0 scatter_custom_fusion
  19.3 405.7 %all-gather.3.cloned.1.call-done = bf16[4096,512]{1,0:T(8,128)(2,1)} async-done(((bf16[16,512]{1,0:T(8,128)(2,1)}), bf16[4096,512]{1,0:T(8,128)(2,1)}) %all-gather.3.cloned.1.call-update) | async-done | bytes 4194320 | tf_op jit(solution)/shard_map/all_gather | solution.py:56
  425.0 2.9 convolution_convert_fusion.12
  427.9 2.0 convolution_convert_fusion.5
  429.9 3.6 all-to-all-start
  435.7 10.0 all-to-all-done
  446.8 2.0 convolution_convert_fusion
  448.8 3.7 all-to-all-start.2
  452.6 3.3 convolution_convert_fusion.1
  455.8 28.8 %all-to-all-done.2 = bf16[16,16,4096]{2,1,0:T(8,128)(2,1)S(1)} async-done(((bf16[16,16,4096]{2,1,0:T(8,128)(2,1)}), bf16[16,16,4096]{2,1,0:T(8,128)(2,1)S(1)}, u32[]{:S(2)}, u32[]{:S(2)}) %all-to-all-start.2) | async-done | bytes 2097184 | tf_op jit(solution)/shard_map/all_to_all | solution.py:94
  484.6 4.4 all-to-all-start.1
  489.5 2.0 fusion.146
  498.5 31.1 %all-to-all-done.1 = bf16[16,16,4096]{2,1,0:T(8,128)(2,1)} async-done(((bf16[16,16,4096]{2,1,0:T(8,128)(2,1)}), bf16[16,16,4096]{2,1,0:T(8,128)(2,1)}, u32[]{:S(2)}, u32[]{:S(2)}) %all-to-all-start.1) | async-done | bytes 2097184 | tf_op jit(solution)/shard_map/all_to_all | solution.py:93
  529.6 2.1 fusion.81
  532.8 2.3 multiply_reduce_fusion
  539.9 2.1 fusion.144
  541.9 4.6 fusion.140
  546.5 4.5 reshape.213
  551.0 4.0 reshape.207
  555.0 8.9 fusion.142
  563.9 4.3 fusion.141
  569.5 3.4 fusion.17
  572.9 3.3 fusion.16
  576.2 2.3 fusion.49
  579.9 3.4 fusion.7
  583.2 2.5 fusion.98
  585.8 4.5 fusion.12
  590.3 2.5 fusion.100
  592.8 4.5 fusion.2
  597.3 6.7 fusion.11
  604.0 2.4 fusion.51
  606.4 6.2 fusion.6
  612.6 4.5 fusion.53
  617.1 4.6 fusion.1
  621.7 1.9 copy-done.6
  623.7 2.3 fusion.55
  625.9 3.8 fusion.68
  629.8 2.7 fusion.71
  632.5 2.6 fusion.74
  635.1 2.7 fusion.77
  637.8 6.4 copy.240
  644.2 85.8 %reduce-scatter.7.cloned.1.call-done = bf16[128,1024]{1,0:T(8,128)(2,1)} async-done(((bf16[2048,1024]{1,0:T(8,128)(2,1)}), bf16[128,1024]{1,0:T(8,128)(2,1)}) %reduce-scatter.7.cloned.1.call-update) | async-done | bytes 262160
  731.4 16.4 all_to_all.20
  748.1 4.5 multiply_bitcast_fusion
  752.6 9.0 copy.242
  761.7 3.4 fusion.83
  765.1 3.7 fusion.85
  772.5 1303.9 %reduce-scatter.9.cloned.1.call-done = f32[16,512]{1,0:T(8,128)} async-done(((f32[4096,512]{1,0:T(8,128)}), f32[16,512]{1,0:T(8,128)}) %reduce-scatter.9.cloned.1.call-update) | async-done | bytes 32784
  (116 shorter events, 28.4 us)
Async XLA Ops:
  7.2 417.8 %copy-start = (bf16[1,128,4096]{2,1,0:T(8,128)(2,1)S(1)}, bf16[1,128,4096]{2,1,0:T(8,128)(2,1)}, u32[]{:S(2)}) copy-start(bf16[1,128,4096]{2,1,0:T(8,128)(2,1)} %param.9) | copy-start | bytes 3145732
  7.2 439.6 %copy-start.21 = (bf16[1,128,4096]{2,1,0:T(8,128)(2,1)S(1)}, bf16[1,128,4096]{2,1,0:T(8,128)(2,1)}, u32[]{:S(2)}) copy-start(bf16[1,128,4096]{2,1,0:T(8,128)(2,1)} %param.14) | copy-start | bytes 3145732
  7.2 417.8 %all-gather.3.cloned.1.call-start = ((), (), s32[]{:S(2)}) async-start(), calls=%async_computation.6 | async-start | bytes 4210688 | tf_op jit(solution)/shard_map/all_gather | solution.py:56
  429.9 15.9 all-to-all-start
  433.4 55.7 %copy-start.28 = (s32[1,8]{1,0:T(1,128)S(1)}, s32[1,8]{1,0:T(1,128)}, u32[]{:S(2)}) copy-start(s32[1,8]{1,0:T(1,128)} %param.15) | copy-start | bytes 100
  433.5 56.1 %copy-start.27 = (s32[1,32,32]{2,1,0:T(8,128)S(1)}, s32[1,32,32]{2,1,0:T(8,128)}, u32[]{:S(2)}) copy-start(s32[1,32,32]{2,1,0:T(8,128)} %param.17) | copy-start | bytes 12292
  433.5 108.5 %all-gather.5.cloned.1.call-start = ((), (), s32[]{:S(2)}) async-start(), calls=%async_computation.7 | async-start | bytes 4456448 | tf_op jit(solution)/shard_map/all_gather | solution.py:100
  448.8 35.8 %all-to-all-start.2 = ((bf16[16,16,4096]{2,1,0:T(8,128)(2,1)}), bf16[16,16,4096]{2,1,0:T(8,128)(2,1)S(1)}, u32[]{:S(2)}, u32[]{:S(2)}) async-start(bf16[16,16,4096]{2,1,0:T(8,128)(2,1)} %bitcast.340), calls=%async_computation.2 | async-start | bytes 4194304 | tf_op jit(solution)/shard_map/all_to_all | solution.py:94
  484.6 6.9 copy-start.8
  484.6 44.9 %all-to-all-start.1 = ((bf16[16,16,4096]{2,1,0:T(8,128)(2,1)}), bf16[16,16,4096]{2,1,0:T(8,128)(2,1)}, u32[]{:S(2)}, u32[]{:S(2)}) async-start(bf16[16,16,4096]{2,1,0:T(8,128)(2,1)} %bitcast.338), calls=%async_computation.1 | async-start | bytes 4194304 | tf_op jit(solution)/shard_map/all_to_all | solution.py:93
  489.1 241.0 %reduce-scatter.7.cloned.1.call-start = ((), (), s32[]{:S(2)}) async-start(), calls=%async_computation.8 | async-start | bytes 4456448
  494.5 85.4 %copy-start.10 = (pred[128,2048]{0,1:T(8,128)(4,1)}, pred[128,2048]{0,1:T(8,128)(4,1)S(1)}, u32[]{:S(2)}) copy-start(pred[128,2048]{0,1:T(8,128)(4,1)S(1)} %copy.165) | copy-start | bytes 786436
  494.5 3.3 copy-start.9
  541.9 36.7 %copy-start.18 = (bf16[128,1,8,128]{3,2,1,0:T(8,128)(2,1)}, bf16[128,1,8,128]{3,2,1,0:T(8,128)(2,1)S(1)}, u32[]{:S(2)}) copy-start(bf16[128,1,8,128]{3,2,1,0:T(8,128)(2,1)S(1)} %get-tuple-element.51) | copy-start | bytes 786436
  555.0 8.9 copy-start.2
  563.9 5.6 copy-start.16
  563.9 14.7 copy-start.14
  568.2 4.6 copy-start.26
  576.2 2.4 copy-start.3
  585.7 4.5 copy-start.1
  597.3 6.7 copy-start.20
  597.3 9.1 copy-start.11
  604.0 8.6 copy-start.4
  606.4 6.2 copy-start.19
  606.4 10.7 copy-start.22
  617.1 6.5 copy-start.17
  621.7 1.9 copy-start.6
  623.7 6.1 slice-start
  623.7 6.1 copy-start.25
  625.9 3.8 slice-start.1
  629.7 2.7 copy-start.24
  632.5 2.6 copy-start.23
  644.2 1432.2 %reduce-scatter.9.cloned.1.call-start = ((), (), s32[]{:S(2)}) async-start(), calls=%async_computation.9 | async-start | bytes 8421376
  761.6 3.5 copy-start.15
  761.6 7.2 copy-start.13
  761.6 7.2 copy-start.5
  761.6 8.0 copy-start.7
  761.6 8.0 copy-start.12
Sparse Core Ops, SparseCore 0:
  9.9 414.9 all-gather.2
  446.9 80.7 all-gather.4
  644.3 85.6 reduce-scatter.6
  761.7 1314.6 reduce-scatter.8
where the time goes:
time: 2090 us; the launch traced here: 2080 us
  waiting for transfers between devices  1870 us (89%)
  matrix products  82 us (4%)
  local copies, waits for them, and re-layouts  67.8 us (3%)
  other arithmetic  24.4 us (1%)
    unnamed x6, waiting for transfers between devices  1390 us
    all_gather x1, waiting for transfers between devices, local(): lax.all_gather(value_weight, ('dp', 'ctx'), axis=0, tiled=True)  406 us
  transfers between devices with their start and end apart: 7, of which 6 were waited for; matrix products, arithmetic and copies ran while one was open for 2% of the time, Pallas kernels for 0%

commit v1 on v0

v1 whole, which is shorter than its diff:
```python
import math

import jax
import jax.numpy as jnp
from jax import lax
from jax.experimental import pallas as pl
from jax.experimental.pallas import tpu as pltpu
from jax.sharding import PartitionSpec as P

HD = 128
VB = 64
ROWS = 128
CTX = 16
CAP = 16
SLOTS = CTX * CAP
GROUP = 8
KVH = 4
Z = 8
D = 4096
KVW = 512
WIN = 1280
USED = 1152
BACK = 4
CHUNK = 256
BF = jnp.bfloat16
F32 = jnp.float32
NT = (((1,), (1,)), ((), ()))
TN = (((0,), (0,)), ((), ()))
SCALE = 1.0 / math.sqrt(HD)


def remote(source, target, send_sem, recv_sem, dp, ctx):
    return pltpu.make_async_remote_copy(
        src_ref=source,
        dst_ref=target,
        send_sem=send_sem,
        recv_sem=recv_sem,
        device_id=(dp, ctx),
        device_id_type=pl.DeviceIdType.MESH,
    )


def rows_at(start, size):
    return pl.ds(pl.multiple_of(start, size), size)


def iota(shape, axis):
    return lax.broadcasted_iota(jnp.int32, shape, axis)


def nt_dot(first, second):
    return lax.dot_general(first, second, NT, preferred_element_type=F32)


def tn_dot(first, second):
    return lax.dot_general(first, second, TN, preferred_element_type=F32)


class Window:
    def __init__(self, own, window, far_send, far_recv, near_send, near_recv, own_sem, dp, ctx):
        self.own, self.window = own, window
        self.far_send, self.far_recv = far_send, far_recv
        self.near_send, self.near_recv = near_send, near_recv
        self.own_sem, self.dp, self.ctx = own_sem, dp, ctx
        self.chip, self.core = ctx // 2, ctx % 2
        self.other = ctx + 1 - 2 * self.core

    def slot(self, back, core):
        return self.window.at[rows_at((8 - 2 * back + core) * ROWS, ROWS)]

    def far(self, back):
        return remote(
            self.own,
            self.slot(back, self.core),
            self.far_send.at[back],
            self.far_recv.at[back],
            self.dp,
            self.ctx + 2 * back,
        )

    def near(self, back, core):
        source = self.own if back == 0 else self.slot(back, core)
        return remote(
            source,
            self.slot(back, core),
            self.near_send.at[back],
            self.near_recv.at[back],
            self.dp,
            self.other,
        )

    def own_copy(self):
        return pltpu.make_async_copy(self.own, self.slot(0, self.core), self.own_sem)

    def start(self):
        for back in range(1, BACK + 1):

            @pl.when(self.chip + back <= 7)
            def _(back=back):
                self.far(back).start()

        self.near(0, self.core).start()
        self.own_copy().start()

    def hand_on(self):
        for back in range(1, BACK + 1):

            @pl.when(self.chip >= back)
            def _(back=back):
                self.far(back).wait_recv()
                self.near(back, self.core).start()

    def finish(self):
        for back in range(BACK + 1):

            @pl.when(self.chip >= back)
            def _(back=back):
                self.near(back, 1 - self.core).wait_recv()
                self.near(back, self.core).wait_send()

        for back in range(1, BACK + 1):

            @pl.when(self.chip + back <= 7)
            def _(back=back):
                self.far(back).wait_send()

        self.own_copy().wait()


class Exchange:
    def __init__(self, source, arrived, send_sem, recv_sem, own_sem, dp, ctx):
        self.source, self.arrived = source, arrived
        self.send_sem, self.recv_sem = send_sem, recv_sem
        self.own_sem, self.dp, self.ctx = own_sem, dp, ctx

    def copy(self, step):
        partner = (self.ctx + step) % CTX
        return remote(
            self.source.at[rows_at(partner * CAP, CAP)],
            self.arrived.at[rows_at(self.ctx * CAP, CAP)],
            self.send_sem.at[step],
            self.recv_sem.at[step],
            self.dp,
            partner,
        )

    def own_copy(self):
        own = rows_at(self.ctx * CAP, CAP)
        return pltpu.make_async_copy(self.source.at[own], self.arrived.at[own], self.own_sem)

    def start(self):
        @pl.loop(1, CTX)
        def _(step):
            self.copy(step).start()

        self.own_copy().start()

    def finish(self):
        @pl.loop(1, CTX)
        def _(step):
            self.copy(step).wait()

        self.own_copy().wait()


def plane_partner(dp, ctx, step):
    chip = ((dp // Z) * 8 + ctx // 2 + step) % 16
    return (chip // 8) * Z + dp % Z, (chip % 8) * 2 + dp // Z


def gather_kernel(
    weight_ref,
    hidden_ref,
    key_ref,
    saved_ref,
    route_ref,
    key_window,
    value_window,
    saved_slots,
    owner_ref,
    pack_ref,
    whole,
    staged,
    value_own,
    empty,
    plane_send,
    plane_recv,
    up_send,
    up_recv,
    down_send,
    down_recv,
    pair_send,
    pair_recv,
    far_send,
    far_recv,
    near_send,
    near_recv,
    slot_send,
    slot_recv,
    own_sems,
):
    dp, ctx = lax.axis_index("dp"), lax.axis_index("ctx")
    x_lo, z = dp // Z, dp % Z
    chip, core = ctx // 2, ctx % 2
    other = ctx + 1 - 2 * core

    shard = whole.at[rows_at((dp * CTX + ctx) * CAP, CAP)]

    def plane_copy(step):
        to_dp, to_ctx = plane_partner(dp, ctx, step)
        return remote(
            weight_ref, shard, plane_send.at[step], plane_recv.at[ctx], to_dp, to_ctx
        )

    own_shard = pltpu.make_async_copy(weight_ref, shard, own_sems.at[3])

    @pl.when(core == x_lo)
    def _():
        own_shard.start()

    @pl.when(core != x_lo)
    def _():
        plane_copy(0).start()

    @pl.loop(1, 16)
    def _(step):
        plane_copy(step).start()

    keys = Window(
        key_ref,
        key_window,
        far_send.at[0],
        far_recv.at[0],
        near_send.at[0],
        near_recv.at[0],
        own_sems.at[0],
        dp,
        ctx,
    )
    values = Window(
        value_own,
        value_window,
        far_send.at[1],
        far_recv.at[1],
        near_send.at[1],
        near_recv.at[1],
        own_sems.at[1],
        dp,
        ctx,
    )
    keys.start()

    route = route_ref[...]
    owner = lax.shift_right_logical(route, 7)
    before = jnp.where(iota((ROWS, ROWS), 0) < iota((ROWS, ROWS), 1), 1.0, 0.0).astype(BF)
    coming = owner == ctx
    rank = jnp.dot(jnp.where(coming, 1.0, 0.0).astype(BF), before, preferred_element_type=F32)
    rank = jnp.where(coming, rank.astype(jnp.int32), -1)
    place = route - ctx * ROWS
    for pack in range(CTX):
        to_rank = jnp.where(rank[pack : pack + 1] == iota((CAP, ROWS), 0), 1.0, 0.0).astype(BF)
        to_place = jnp.where(place[pack : pack + 1] == iota((ROWS, ROWS), 0), 1.0, 0.0).astype(BF)
        owner_ref[pack * CAP : (pack + 1) * CAP] = nt_dot(to_rank, to_place).astype(BF)
    for part in range(4):
        columns = slice(part * 1024, (part + 1) * 1024)
        staged[:, columns] = jnp.dot(
            owner_ref[...], saved_ref[:, columns], preferred_element_type=F32
        ).astype(BF)
    saved_exchange = Exchange(staged, saved_slots, slot_send, slot_recv, own_sems.at[2], dp, ctx)
    saved_exchange.start()

    own_owner = lax.shift_right_logical(route_ref[pl.ds(ctx, 1)], 7)
    hit = own_owner == iota((CTX, ROWS), 0)
    count = jnp.dot(jnp.where(hit, 1.0, 0.0).astype(BF), before, preferred_element_type=F32)
    own_rank = jnp.sum(jnp.where(hit, count, 0.0), axis=0, keepdims=True).astype(jnp.int32)
    pack_ref[...] = jnp.where(
        own_owner * CAP + own_rank == iota((SLOTS, ROWS), 0), 1.0, 0.0
    ).astype(BF)

    empty[...] = jnp.zeros_like(empty)
    for back in range(1, BACK + 1):

        @pl.when(chip < back)
        def _(back=back):
            hole = pl.ds((8 - 2 * back) * ROWS, 2 * ROWS)
            pltpu.sync_copy(empty, key_window.at[hole])
            pltpu.sync_copy(empty, value_window.at[hole])

    @pl.when(core == x_lo)
    def _():
        own_shard.wait()

    @pl.loop(0, CTX)
    def _(source):
        @pl.when(jnp.logical_or(core != x_lo, source != ctx))
        def _():
            shard_in = whole.at[rows_at(((core * Z + z) * CTX + source) * CAP, CAP)]
            remote(
                weight_ref, shard_in, plane_send.at[0], plane_recv.at[source], dp, other
            ).wait_recv()

    def chunk(at_core, at_z, half):
        start = (at_core * Z + at_z) * CHUNK
        if half is None:
            return whole.at[rows_at(start, CHUNK)]
        return whole.at[rows_at(start + half * (CHUNK // 2), CHUNK // 2)]

    def up(step, half=None):
        block = chunk(core, (z + Z - step) % Z, half)
        return remote(block, block, up_send.at[step], up_recv.at[step], x_lo * Z + (z + 1) % Z, ctx)

    def down(step, half=None):
        block = chunk(core, (z + step) % Z, half)
        return remote(
            block, block, down_send.at[step], down_recv.at[step], x_lo * Z + (z + Z - 1) % Z, ctx
        )

    def up_in(step, half=None):
        block = chunk(core, (z + Z - step - 1) % Z, half)
        return remote(
            block, block, up_send.at[step], up_recv.at[step], x_lo * Z + (z + 1) % Z, ctx
        )

    def down_in(step, half=None):
        block = chunk(core, (z + step + 1) % Z, half)
        return remote(
            block, block, down_send.at[step], down_recv.at[step], x_lo * Z + (z + Z - 1) % Z, ctx
        )

    def pair(index, at_core):
        offset, half = ((0, None), (-1, None), (1, None), (-2, None), (2, None), (-3, None), (3, None), (4, 0), (4, 1))[index]
        block = chunk(at_core, (z + Z + offset) % Z, half)
        return remote(block, block, pair_send.at[index], pair_recv.at[index], dp, other)

    up(0).start()
    down(0).start()
    pair(0, core).start()
    keys.hand_on()
    for step in range(3):
        up_in(step).wait_recv()
        if step < 2:
            up(step + 1).start()
        else:
            up(3, 0).start()
        pair(2 * step + 1, core).start()
        down_in(step).wait_recv()
        if step < 2:
            down(step + 1).start()
        else:
            down(3, 1).start()
        pair(2 * step + 2, core).start()
    up_in(3, 0).wait_recv()
    pair(7, core).start()
    down_in(3, 1).wait_recv()
    pair(8, core).start()
    for index in range(9):
        pair(index, 1 - core).wait_recv()
    value_own[...] = jnp.dot(hidden_ref[...], whole[...], preferred_element_type=F32).astype(BF)
    values.start()
    values.hand_on()

    for step in range(3):
        up(step).wait_send()
        down(step).wait_send()
    up(3, 0).wait_send()
    down(3, 1).wait_send()
    for index in range(9):
        pair(index, core).wait_send()

    @pl.when(core != x_lo)
    def _():
        plane_copy(0).wait_send()

    @pl.loop(1, 16)
    def _(step):
        plane_copy(step).wait_send()

    keys.finish()
    values.finish()
    saved_exchange.finish()


def gather(weight, hidden, keys, saved, route):
    vmem = pl.BlockSpec(memory_space=pltpu.VMEM)
    hbm = pl.BlockSpec(memory_space=pl.ANY)
    dma = pltpu.SemaphoreType.DMA
    return pl.pallas_call(
        gather_kernel,
        out_shape=(
            jax.ShapeDtypeStruct((WIN, KVW), BF),
            jax.ShapeDtypeStruct((WIN, KVW), BF),
            jax.ShapeDtypeStruct((SLOTS, D), BF),
            jax.ShapeDtypeStruct((SLOTS, ROWS), BF),
            jax.ShapeDtypeStruct((SLOTS, ROWS), BF),
        ),
        in_specs=[vmem] * 5,
        out_specs=(hbm, hbm, hbm, vmem, vmem),
        scratch_shapes=[
            pltpu.VMEM((D, KVW), BF),
            pltpu.VMEM((SLOTS, D), BF),
            pltpu.VMEM((ROWS, KVW), BF),
            pltpu.VMEM((2 * ROWS, KVW), BF),
            dma((16,)),
            dma((16,)),
            dma((4,)),
            dma((4,)),
            dma((4,)),
            dma((4,)),
            dma((9,)),
            dma((9,)),
            dma((2, BACK + 1)),
            dma((2, BACK + 1)),
            dma((2, BACK + 1)),
            dma((2, BACK + 1)),
            dma((CTX,)),
            dma((CTX,)),
            dma((4,)),
        ],
        compiler_params=pltpu.CompilerParams(
            has_side_effects=True, vmem_limit_bytes=40 * 1024 * 1024
        ),
        name="gather_inputs",
    )(weight, hidden, keys, saved, route)


def attention_kernel(
    length_ref,
    visible_ref,
    query_ref,
    grad_ref,
    saved_ref,
    key_ref,
    value_ref,
    pack_ref,
    staged_ref,
    terms_ref,
    bias,
    queries,
    grads,
    weights_all,
    dscores_all,
):
    ctx = lax.axis_index("ctx")
    core = ctx % 2

    @pl.when(pl.program_id(0) == 0)
    def _():
        position = ctx * ROWS + iota((1, ROWS), 1)
        start = jnp.zeros((1, ROWS), jnp.int32)
        end = jnp.int32(0)
        for n in range(8):
            length = length_ref[0, n]
            end = end + length
            start = start + jnp.where(position >= end, length, 0)
        left = iota((1, ROWS), 1) < VB
        for block in range(USED // VB):
            column = jnp.maximum(2 * ctx - 16 + block, 0)
            seen = jnp.where(left, visible_ref[2 * ctx, column], visible_ref[2 * ctx + 1, column])
            key_position = ctx * ROWS - 1024 + block * VB + iota((VB, ROWS), 0)
            allowed = (key_position >= start) & (key_position <= position) & (seen == 1)
            bias[block * VB : (block + 1) * VB] = jnp.where(allowed, 0.0, -1e30)

    for head in range(GROUP):
        columns = slice(head * HD, (head + 1) * HD)
        queries[columns] = query_ref[:, columns]
        grads[columns] = grad_ref[:, columns]
    product = tn_dot(pack_ref[...], saved_ref[...]) * grad_ref[...].astype(F32)
    high = product.astype(BF)
    low = (product - high.astype(F32)).astype(BF)
    heads = jnp.where(
        lax.shift_right_logical(iota((GROUP, GROUP * HD), 1), 7) == iota((GROUP, GROUP * HD), 0),
        1.0,
        0.0,
    ).astype(BF)
    delta = nt_dot(heads, high) + nt_dot(heads, low)
    used = pl.ds(pl.multiple_of(core * ROWS, ROWS), USED)
    keys = key_ref[used]
    values = value_ref[used]
    mask = bias[...]
    for head in range(GROUP):
        columns = slice(head * HD, (head + 1) * HD)
        scores = nt_dot(keys, queries[columns]) + mask
        top = jnp.max(scores, axis=0, keepdims=True)
        raised = jnp.exp((scores - top) * SCALE)
        weights = raised * (1.0 / jnp.sum(raised, axis=0, keepdims=True))
        weights_all[:, columns] = weights.astype(BF)
        dweights = nt_dot(values, grads[columns]).astype(BF).astype(F32)
        dscores_all[:, columns] = (
            (weights * SCALE) * (dweights - delta[head : head + 1])
        ).astype(BF)
    unused = pl.ds(pl.multiple_of((1 - core) * USED, ROWS), ROWS)
    terms_ref[unused] = jnp.zeros((ROWS, 2 * HD), BF)
    terms_ref[used, :HD] = jnp.dot(
        dscores_all[...], queries[...], preferred_element_type=F32
    ).astype(BF)
    terms_ref[used, HD:] = jnp.dot(
        weights_all[...], grads[...], preferred_element_type=F32
    ).astype(BF)
    query_grad = tn_dot(keys, dscores_all[...]).astype(BF)
    for head in range(GROUP):
        columns = slice(head * HD, (head + 1) * HD)
        staged_ref[:, columns] = nt_dot(pack_ref[...], query_grad[:, columns]).astype(BF)


def attention(lengths, visible, queries, grads, saved_slots, key_window, value_window, pack):
    smem = pl.BlockSpec(memory_space=pltpu.SMEM)
    width = GROUP * HD

    def by_group(rows, columns):
        return pl.BlockSpec((rows, columns), lambda g: (0, g))

    return pl.pallas_call(
        attention_kernel,
        grid=(KVH,),
        out_shape=(
            jax.ShapeDtypeStruct((SLOTS, D), BF),
            jax.ShapeDtypeStruct((WIN, 2 * KVW), BF),
        ),
        in_specs=[
            smem,
            smem,
            by_group(ROWS, width),
            by_group(ROWS, width),
            by_group(SLOTS, width),
            by_group(WIN, HD),
            by_group(WIN, HD),
            pl.BlockSpec((SLOTS, ROWS), lambda g: (0, 0)),
        ],
        out_specs=(by_group(SLOTS, width), by_group(WIN, 2 * HD)),
        scratch_shapes=[
            pltpu.VMEM((USED, ROWS), F32),
            pltpu.VMEM((GROUP * HD, HD), BF),
            pltpu.VMEM((GROUP * HD, HD), BF),
            pltpu.VMEM((USED, GROUP * HD), BF),
            pltpu.VMEM((USED, GROUP * HD), BF),
        ],
        compiler_params=pltpu.CompilerParams(vmem_limit_bytes=48 * 1024 * 1024),
        name="attention_backward",
    )(lengths, visible, queries, grads, saved_slots, key_window, value_window, pack)


def reduce_kernel(
    terms_ref,
    staged_ref,
    hidden_ref,
    owner_ref,
    query_grad_ref,
    key_grad_ref,
    weight_grad_ref,
    near_in,
    far_out,
    far_in,
    total,
    value_grad,
    query_slots,
    mine,
    theirs,
    from_pair,
    up_in,
    down_in,
    up_out,
    down_out,
    plane_in,
    near_send,
    near_recv,
    far_send,
    far_recv,
    slot_send,
    slot_recv,
    own_sem,
    pair_send,
    pair_recv,
    up_send,
    up_recv,
    down_send,
    down_recv,
    plane_send,
    plane_recv,
):
    dp, ctx = lax.axis_index("dp"), lax.axis_index("ctx")
    x_lo, z = dp // Z, dp % Z
    chip, core = ctx // 2, ctx % 2
    other = ctx + 1 - 2 * core

    def block_of(back, at_core):
        return rows_at((8 - 2 * back + at_core) * ROWS, ROWS)

    def near(back):
        return remote(
            terms_ref.at[block_of(back, 1 - core)],
            near_in.at[back],
            near_send.at[back],
            near_recv.at[back],
            dp,
            other,
        )

    def far(back):
        return remote(
            far_out.at[back],
            far_in.at[back],
            far_send.at[back],
            far_recv.at[back],
            dp,
            ctx - 2 * back,
        )

    for back in (1, 2, 3, 4, 0):

        @pl.when(chip >= back)
        def _(back=back):
            near(back).start()

    for back in range(1, BACK + 1):

        @pl.when(chip >= back)
        def _(back=back):
            near(back).wait_recv()
            far_out[back] = (
                terms_ref[block_of(back, core)].astype(F32) + near_in[back].astype(F32)
            ).astype(BF)
            far(back).start()

    query_exchange = Exchange(staged_ref, query_slots, slot_send, slot_recv, own_sem, dp, ctx)
    query_exchange.start()
    near(0).wait_recv()
    total[...] = terms_ref[block_of(0, core)].astype(F32) + near_in[0].astype(F32)
    for back in range(1, BACK + 1):

        @pl.when(chip + back <= 7)
        def _(back=back):
            far(back).wait_recv()
            total[...] += far_in[back].astype(F32)

    for group in range(KVH):
        columns = slice(group * HD, (group + 1) * HD)
        key_grad_ref[:, columns] = total[:, group * 2 * HD : group * 2 * HD + HD].astype(BF)
        value_grad[:, columns] = total[:, group * 2 * HD + HD : (group + 1) * 2 * HD].astype(BF)

    offsets = (4, 3, -3, 2, -2, 1, -1, 0)

    def partial_at(at_core, offset):
        start = (at_core * Z + (z + Z + offset) % Z) * CHUNK
        return tn_dot(hidden_ref[:, rows_at(start, CHUNK)], value_grad[...])

    def pair(index):
        return remote(
            theirs.at[index],
            from_pair.at[index],
            pair_send.at[index],
            pair_recv.at[index],
            dp,
            other,
        )

    for index, offset in enumerate(offsets):
        theirs[index] = partial_at(1 - core, offset).astype(BF)
        pair(index).start()
    for index, offset in enumerate(offsets):
        mine[index] = partial_at(core, offset).astype(BF)

    half = CHUNK // 2
    above, below = x_lo * Z + (z + 1) % Z, x_lo * Z + (z + Z - 1) % Z

    def up(step):
        source, target = up_out.at[step], up_in.at[step]
        if step == 0:
            source, target = source.at[pl.ds(0, half)], target.at[pl.ds(0, half)]
        return remote(source, target, up_send.at[step], up_recv.at[step], above, ctx)

    def down(step):
        source, target = down_out.at[step], down_in.at[step]
        if step == 0:
            source, target = source.at[pl.ds(half, half)], target.at[pl.ds(half, half)]
        return remote(source, target, down_send.at[step], down_recv.at[step], below, ctx)

    def chip_sum(index):
        return mine[index].astype(F32) + from_pair[index].astype(F32)

    pair(0).wait_recv()
    furthest = chip_sum(0).astype(BF)
    up_out[0, :half] = furthest[:half]
    down_out[0, half:] = furthest[half:]
    up(0).start()
    down(0).start()
    for step in range(1, 4):
        for index, ring, out, arrived, kept in (
            (2 * step - 1, up, up_out, up_in, slice(0, half)),
            (2 * step, down, down_out, down_in, slice(half, CHUNK)),
        ):
            pair(index).wait_recv()
            out[step] = chip_sum(index).astype(BF)
            ring(step - 1).wait_recv()
            if step == 1:
                out[step, kept] = (
                    chip_sum(index)[kept] + arrived[step - 1, kept].astype(F32)
                ).astype(BF)
            else:
                out[step] = (chip_sum(index) + arrived[step - 1].astype(F32)).astype(BF)
            ring(step).start()
    pair(7).wait_recv()
    up(3).wait_recv()
    down(3).wait_recv()
    mine[7] = (chip_sum(7) + up_in[3].astype(F32) + down_in[3].astype(F32)).astype(BF)

    plane = (dp // Z) * 8 + chip

    def plane_copy(step):
        to_ctx = (ctx + step) % CTX
        return remote(
            mine.at[7, rows_at(to_ctx * CAP, CAP)],
            plane_in.at[plane],
            plane_send.at[step],
            plane_recv.at[plane],
            core * Z + z,
            to_ctx,
        )

    own_plane = pltpu.make_async_copy(
        mine.at[7, rows_at(ctx * CAP, CAP)], plane_in.at[plane], own_sem
    )

    query_exchange.finish()

    @pl.when(core == x_lo)
    def _():
        own_plane.start()

    @pl.when(core != x_lo)
    def _():
        plane_copy(0).start()

    @pl.loop(1, CTX)
    def _(step):
        plane_copy(step).start()

    for part in range(4):
        columns = slice(part * 1024, (part + 1) * 1024)
        query_grad_ref[:, columns] = tn_dot(owner_ref[...], query_slots[:, columns]).astype(BF)

    @pl.when(core == x_lo)
    def _():
        own_plane.wait()

    @pl.loop(0, 16)
    def _(source):
        @pl.when(jnp.logical_or(core != x_lo, source != plane))
        def _():
            remote(
                mine.at[7, pl.ds(0, CAP)],
                plane_in.at[source],
                plane_send.at[0],
                plane_recv.at[source],
                dp,
                other,
            ).wait_recv()

    weight_sum = plane_in[0].astype(F32)
    for source in range(1, 16):
        weight_sum = weight_sum + plane_in[source].astype(F32)
    weight_grad_ref[...] = weight_sum * (1.0 / math.sqrt(32768.0))

    @pl.when(core != x_lo)
    def _():
        plane_copy(0).wait_send()

    @pl.loop(1, CTX)
    def _(step):
        plane_copy(step).wait_send()

    for step in range(4):
        up(step).wait_send()
        down(step).wait_send()
    for index in range(8):
        pair(index).wait_send()
    for back in range(BACK + 1):

        @pl.when(chip >= back)
        def _(back=back):
            near(back).wait_send()
            if back > 0:
                far(back).wait_send()


def reduce(terms, staged, hidden, owner):
    vmem = pl.BlockSpec(memory_space=pltpu.VMEM)
    hbm = pl.BlockSpec(memory_space=pl.ANY)
    dma = pltpu.SemaphoreType.DMA
    chunk = (CHUNK, KVW)
    return pl.pallas_call(
        reduce_kernel,
        out_shape=(
            jax.ShapeDtypeStruct((ROWS, D), BF),
            jax.ShapeDtypeStruct((ROWS, KVW), BF),
            jax.ShapeDtypeStruct((CAP, KVW), F32),
        ),
        in_specs=[vmem, hbm, vmem, vmem],
        out_specs=(vmem, vmem, vmem),
        scratch_shapes=[
            pltpu.VMEM((BACK + 1, ROWS, 2 * KVW), BF),
            pltpu.VMEM((BACK + 1, ROWS, 2 * KVW), BF),
            pltpu.VMEM((BACK + 1, ROWS, 2 * KVW), BF),
            pltpu.VMEM((ROWS, 2 * KVW), F32),
            pltpu.VMEM((ROWS, KVW), BF),
            pltpu.VMEM((SLOTS, D), BF),
            pltpu.VMEM((8,) + chunk, BF),
            pltpu.VMEM((8,) + chunk, BF),
            pltpu.VMEM((8,) + chunk, BF),
            pltpu.VMEM((4,) + chunk, BF),
            pltpu.VMEM((4,) + chunk, BF),
            pltpu.VMEM((4,) + chunk, BF),
            pltpu.VMEM((4,) + chunk, BF),
            pltpu.VMEM((16, CAP, KVW), BF),
            dma((BACK + 1,)),
            dma((BACK + 1,)),
            dma((BACK + 1,)),
            dma((BACK + 1,)),
            dma((CTX,)),
            dma((CTX,)),
            dma,
            dma((8,)),
            dma((8,)),
            dma((4,)),
            dma((4,)),
            dma((4,)),
            dma((4,)),
            dma((16,)),
            dma((16,)),
        ],
        compiler_params=pltpu.CompilerParams(
            has_side_effects=True, vmem_limit_bytes=48 * 1024 * 1024
        ),
        name="reduce_gradients",
    )(terms, staged, hidden, owner)


def local(
    hidden,
    value_weight,
    queries,
    key_rows,
    attn_saved,
    grad_out,
    doc_lengths,
    routing,
    visible_blocks,
):
    key_window, value_window, saved_slots, owner, pack = gather(
        value_weight, hidden[0], key_rows[0], attn_saved[0], routing.reshape(CTX, ROWS)
    )
    staged, terms = attention(
        doc_lengths,
        visible_blocks[0],
        queries[0],
        grad_out[0],
        saved_slots,
        key_window,
        value_window,
        pack,
    )
    grad_query, grad_key, grad_weight = reduce(terms, staged, hidden[0], owner)
    return (grad_query[None], grad_key[None], grad_weight)


def solution(mesh):
    return jax.shard_map(
        local,
        mesh=mesh,
        in_specs=(
            P("dp", "ctx", None),
            P(("dp", "ctx"), None),
            P("dp", "ctx", None),
            P("dp", "ctx", None),
            P("dp", "ctx", None),
            P("dp", "ctx", None),
            P("dp", None),
            P("dp", None),
            P("dp", None, None),
        ),
        out_specs=(P("dp", "ctx", None), P("dp", "ctx", None), P(("dp", "ctx"), None)),
        check_vma=False,
    )
```

time: 2090 us -> 189 us (0.09)
  the two profiles are of different devices: /device:TPU:128 before, /device:TPU:1 now
where the time goes in v1:
time: 189 us; the launch traced here: 188 us
  Pallas kernels  178 us (94%)
  local copies, waits for them, and re-layouts  9.94 us (5%)
    pallas_call x1, Pallas kernels, reduce(): pl.pallas_call(reduce_kernel, out_shape=(jax.ShapeDtypeStruct((ROWS, D),...  83.6 us
    pallas_call x1, Pallas kernels, gather(): pl.pallas_call(gather_kernel, out_shape=(jax.ShapeDtypeStruct((WIN, KVW),...  65.6 us
    pallas_call x1, Pallas kernels, attention(): pl.pallas_call(attention_kernel, grid=(KVH,), out_shape=(jax.ShapeDtypeSt...  28.4 us
    unnamed x27, local copies, waits for them, and re-layouts  9.94 us

profile of v1, /device:TPU:1, one launch (start us, length us, event | category | flops | bytes accessed | tf_op | source)
XLA Modules:
  0.0 188.3 jit_solution(12984496756359638693)
XLA Ops:
  0.6 0.0 copy-start.11
  0.6 0.0 copy-start
  0.7 1.2 copy-done
  1.9 0.0 copy-start.4
  1.9 1.2 copy-done.4
  3.1 0.0 copy-start.7
  3.1 0.9 copy-done.7
  4.0 0.0 copy-start.8
  4.0 0.7 copy-done.8
  4.7 0.0 copy-start.10
  4.7 0.7 copy-done.10
  5.4 0.0 copy-start.5
  5.4 0.0 copy-start.6
  5.4 0.0 copy-start.9
  5.4 65.6 %gather_inputs.1 = (bf16[1280,512]{1,0:T(8,128)(2,1)S(1)}, bf16[1280,512]{1,0:T(8,128)(2,1)S(1)}, bf16[256,4096]{1,0:T(8,128)(2,1)S(1)}, bf16[256,128]{1,0:T(8,128)(2,1)S(1)}, bf16[256,128]{1,0:T(8,128)(2,1)S(1)}) custom-call(bf16[16,512]{1,0:T(8,128)(2,1)S(1)} %copy-done.8, bf16[128,4096]{1,0:T(8,128)(2,1)S(1)} %bitcast.9, bf16[128,512]{1,0:T(8,128)(2,1)S(1)} %bitcast.15, ...), custom_call_target="tpu_custom_call" | custom-call | tf_op jit(solution)/shard_map/gather_inputs/pallas_call | solution.py:387
  71.1 0.0 copy-start.2
  71.1 1.3 copy-done.2
  72.4 0.0 copy-done.11
  72.4 0.0 copy-done.5
  72.4 0.0 copy-done.6
  72.4 0.0 copy-done.9
  72.4 0.0 copy-start.1
  72.4 28.4 %attention_backward.1 = (bf16[256,4096]{1,0:T(8,128)(2,1)}, bf16[1280,1024]{1,0:T(8,128)(2,1)}) custom-call(s32[1,8]{1,0:T(1,128)S(1)} %copy-done.11, s32[32,32]{1,0:T(8,128)S(1)} %bitcast.17, bf16[128,4096]{1,0:T(8,128)(2,1)S(1)} %bitcast.13, bf16[128,4096]{1,0:T(8,128)(2,1)S(1)} %bitcast.14, bf16[256,4096]{1,0:T(8,128)(2,1)} %copy-done.2, ...), custom_call_target="tpu_custom_call" | custom-call | tf_op jit(solution)/shard_map/attention_backward/pallas_call | solution.py:512
  100.8 0.0 copy-done.1
  100.8 0.0 copy-start.3
  100.8 1.6 copy-done.3
  102.4 83.6 %reduce_gradients.1 = (bf16[128,4096]{1,0:T(8,128)(2,1)S(1)}, bf16[128,512]{1,0:T(8,128)(2,1)S(1)}, f32[16,512]{1,0:T(8,128)S(1)}) custom-call(bf16[1280,1024]{1,0:T(8,128)(2,1)} %get-tuple-element.17.terms_ref, bf16[256,4096]{1,0:T(8,128)(2,1)S(1)} %copy-done.3, bf16[128,4096]{1,0:T(8,128)(2,1)S(1)} %bitcast.10, ...), custom_call_target="tpu_custom_call" | custom-call | tf_op jit(solution)/shard_map/reduce_gradients/pallas_call | solution.py:790
  186.0 1.0 copy.15
  187.0 0.7 copy.16
  187.6 0.6 copy.17
Async XLA Ops:
  0.6 71.8 %copy-start.11 = (s32[1,8]{1,0:T(1,128)S(1)}, s32[1,8]{1,0:T(1,128)}, u32[]{:S(2)}) copy-start(s32[1,8]{1,0:T(1,128)} %length_ref.1) | copy-start | bytes 100
  0.6 1.2 copy-start
  1.9 1.2 copy-start.4
  3.1 0.9 copy-start.7
  4.0 0.7 copy-start.8
  4.7 0.7 copy-start.10
  5.4 67.0 %copy-start.5 = (bf16[1,128,4096]{2,1,0:T(8,128)(2,1)S(1)}, bf16[1,128,4096]{2,1,0:T(8,128)(2,1)}, u32[]{:S(2)}) copy-start(bf16[1,128,4096]{2,1,0:T(8,128)(2,1)} %param.11) | copy-start | bytes 3145732
  5.4 67.0 %copy-start.6 = (bf16[1,128,4096]{2,1,0:T(8,128)(2,1)S(1)}, bf16[1,128,4096]{2,1,0:T(8,128)(2,1)}, u32[]{:S(2)}) copy-start(bf16[1,128,4096]{2,1,0:T(8,128)(2,1)} %param.14) | copy-start | bytes 3145732
  5.4 67.0 %copy-start.9 = (s32[1,32,32]{2,1,0:T(8,128)S(1)}, s32[1,32,32]{2,1,0:T(8,128)}, u32[]{:S(2)}) copy-start(s32[1,32,32]{2,1,0:T(8,128)} %param.17) | copy-start | bytes 12292
  71.1 1.3 copy-start.2
  72.4 28.4 %copy-start.1 = (bf16[1,128,4096]{2,1,0:T(8,128)(2,1)S(1)}, bf16[1,128,4096]{2,1,0:T(8,128)(2,1)}, u32[]{:S(2)}) copy-start(bf16[1,128,4096]{2,1,0:T(8,128)(2,1)} %param.9) | copy-start | bytes 3145732
  100.8 1.6 copy-start.3

commit v2 on v0

v2 whole, which is shorter than its diff:
```python
import math

import jax
import jax.numpy as jnp
from jax import lax
from jax.experimental import pallas as pl
from jax.experimental.pallas import tpu as pltpu
from jax.sharding import PartitionSpec as P

QH = 32
HD = 128
VB = 64
ROWS = 128
CTX = 16
CAP = 16
SLOTS = CTX * CAP
GROUP = 8
KVH = 4
Z = 8
D = 4096
KVW = 512
WIN = 1280
USED = 1152
BACK = 4
CHUNK = 256
BF = jnp.bfloat16
F32 = jnp.float32
NT = (((1,), (1,)), ((), ()))
TN = (((0,), (0,)), ((), ()))
SCALE = 1.0 / math.sqrt(HD)


def remote(source, target, send_sem, recv_sem, dp, ctx):
    return pltpu.make_async_remote_copy(
        src_ref=source,
        dst_ref=target,
        send_sem=send_sem,
        recv_sem=recv_sem,
        device_id=(dp, ctx),
        device_id_type=pl.DeviceIdType.MESH,
    )


def rows_at(start, size):
    return pl.ds(pl.multiple_of(start, size), size)


def iota(shape, axis):
    return lax.broadcasted_iota(jnp.int32, shape, axis)


def nt_dot(first, second):
    return lax.dot_general(first, second, NT, preferred_element_type=F32)


def tn_dot(first, second):
    return lax.dot_general(first, second, TN, preferred_element_type=F32)


class Window:
    def __init__(self, own, window, far_send, far_recv, near_send, near_recv, own_sem, dp, ctx):
        self.own, self.window = own, window
        self.far_send, self.far_recv = far_send, far_recv
        self.near_send, self.near_recv = near_send, near_recv
        self.own_sem, self.dp, self.ctx = own_sem, dp, ctx
        self.chip, self.core = ctx // 2, ctx % 2
        self.other = ctx + 1 - 2 * self.core

    def slot(self, back, core):
        return self.window.at[rows_at((8 - 2 * back + core) * ROWS, ROWS)]

    def far(self, back):
        return remote(
            self.own,
            self.slot(back, self.core),
            self.far_send.at[back],
            self.far_recv.at[back],
            self.dp,
            self.ctx + 2 * back,
        )

    def near(self, back, core):
        source = self.own if back == 0 else self.slot(back, core)
        return remote(
            source,
            self.slot(back, core),
            self.near_send.at[back],
            self.near_recv.at[back],
            self.dp,
            self.other,
        )

    def own_copy(self):
        return pltpu.make_async_copy(self.own, self.slot(0, self.core), self.own_sem)

    def start(self):
        for back in range(1, BACK + 1):

            @pl.when(self.chip + back <= 7)
            def _(back=back):
                self.far(back).start()

        self.near(0, self.core).start()
        self.own_copy().start()

    def hand_on(self):
        for back in range(1, BACK + 1):

            @pl.when(self.chip >= back)
            def _(back=back):
                self.far(back).wait_recv()
                self.near(back, self.core).start()

    def arrive(self):
        for back in range(BACK + 1):

            @pl.when(self.chip >= back)
            def _(back=back):
                self.near(back, 1 - self.core).wait_recv()

        self.own_copy().wait()

    def finish(self):
        for back in range(BACK + 1):

            @pl.when(self.chip >= back)
            def _(back=back):
                self.near(back, self.core).wait_send()

        for back in range(1, BACK + 1):

            @pl.when(self.chip + back <= 7)
            def _(back=back):
                self.far(back).wait_send()


class Terms:
    def __init__(self, terms, near_in, far_out, far_in, total, sems, dp, ctx, columns):
        self.terms, self.near_in = terms, near_in
        self.far_out, self.far_in, self.total = far_out, far_in, total
        self.sems, self.dp, self.ctx, self.columns = sems, dp, ctx, columns
        self.chip, self.core = ctx // 2, ctx % 2
        self.other = ctx + 1 - 2 * self.core

    def block(self, back, core):
        return rows_at((8 - 2 * back + core) * ROWS, ROWS)

    def near(self, back):
        return remote(
            self.terms.at[self.block(back, 1 - self.core), self.columns],
            self.near_in.at[back, :, self.columns],
            self.sems[0].at[back],
            self.sems[1].at[back],
            self.dp,
            self.other,
        )

    def far(self, back):
        return remote(
            self.far_out.at[back, :, self.columns],
            self.far_in.at[back, :, self.columns],
            self.sems[2].at[back],
            self.sems[3].at[back],
            self.dp,
            self.ctx - 2 * back,
        )

    def start(self):
        for back in (4, 3, 2, 1, 0):

            @pl.when(self.chip >= back)
            def _(back=back):
                self.near(back).start()

    def pair_sum(self, back):
        own = self.terms[self.block(back, self.core), self.columns]
        return own.astype(F32) + self.near_in[back, :, self.columns].astype(F32)

    def send(self):
        for back in (4, 3, 2, 1):

            @pl.when(self.chip >= back)
            def _(back=back):
                self.near(back).wait_recv()
                self.far_out[back, :, self.columns] = self.pair_sum(back).astype(BF)
                self.far(back).start()

        self.near(0).wait_recv()
        self.total[:, self.columns] = self.pair_sum(0)

    def add(self):
        for back in range(1, BACK + 1):

            @pl.when(self.chip + back <= 7)
            def _(back=back):
                self.far(back).wait_recv()
                self.total[:, self.columns] += self.far_in[back, :, self.columns].astype(F32)

    def finish(self):
        for back in range(BACK + 1):

            @pl.when(self.chip >= back)
            def _(back=back):
                self.near(back).wait_send()
                if back > 0:
                    self.far(back).wait_send()


class Exchange:
    def __init__(self, source, arrived, send_sem, recv_sem, own_sem, dp, ctx, columns):
        self.source, self.arrived = source, arrived
        self.send_sem, self.recv_sem = send_sem, recv_sem
        self.own_sem, self.dp, self.ctx, self.columns = own_sem, dp, ctx, columns

    def copy(self, step):
        partner = (self.ctx + step) % CTX
        return remote(
            self.source.at[rows_at(partner * CAP, CAP), self.columns],
            self.arrived.at[rows_at(self.ctx * CAP, CAP), self.columns],
            self.send_sem.at[step],
            self.recv_sem.at[step],
            self.dp,
            partner,
        )

    def own_copy(self):
        own = rows_at(self.ctx * CAP, CAP)
        return pltpu.make_async_copy(
            self.source.at[own, self.columns], self.arrived.at[own, self.columns], self.own_sem
        )

    def start(self):
        @pl.loop(1, CTX)
        def _(step):
            self.copy(step).start()

        self.own_copy().start()

    def finish(self):
        @pl.loop(1, CTX)
        def _(step):
            self.copy(step).wait()

        self.own_copy().wait()


def plane_partner(dp, ctx, step):
    chip = ((dp // Z) * 8 + ctx // 2 + step) % 16
    return (chip // 8) * Z + dp % Z, (chip % 8) * 2 + dp // Z


def one_hot(rows, shape):
    return jnp.where(rows == iota(shape, 0), 1.0, 0.0).astype(BF)


def kernel(
    length_ref,
    visible_ref,
    weight_ref,
    hidden_hbm,
    key_ref,
    saved_hbm,
    route_ref,
    query_hbm,
    grad_hbm,
    query_grad_ref,
    key_grad_ref,
    weight_grad_ref,
    hidden_ref,
    turned,
    queries,
    grads,
    saved_ref,
    staged,
    saved_slots,
    owner_turned,
    pack_ref,
    pack_turned,
    bias,
    delta,
    whole,
    value_own,
    empty,
    key_window,
    value_window,
    weights_all,
    dscores_all,
    key_terms,
    value_terms,
    staged_grad,
    query_slots,
    near_in,
    far_out,
    far_in,
    totals,
    value_grad,
    mine,
    theirs,
    from_pair,
    up_in,
    down_in,
    up_out,
    down_out,
    plane_in,
    load_sems,
    head_sems,
    own_sems,
    plane_sems,
    ring_sems,
    pair_sems,
    window_sems,
    slot_sems,
    term_sems,
    query_sems,
    pair_back_sems,
    ring_back_sems,
    plane_back_sems,
):
    dp, ctx = lax.axis_index("dp"), lax.axis_index("ctx")
    x_lo, z = dp // Z, dp % Z
    chip, core = ctx // 2, ctx % 2
    other = ctx + 1 - 2 * core
    above, below = x_lo * Z + (z + 1) % Z, x_lo * Z + (z + Z - 1) % Z

    load_saved = pltpu.make_async_copy(saved_hbm, saved_ref, load_sems.at[0])
    load_hidden = pltpu.make_async_copy(hidden_hbm, hidden_ref, load_sems.at[1])

    def load_query(head):
        columns = pl.ds(pl.multiple_of(head * HD, HD), HD)
        return pltpu.make_async_copy(
            query_hbm.at[:, columns], queries.at[rows_at(head * HD, HD)], head_sems.at[0, head]
        )

    def load_grad(head):
        columns = pl.ds(pl.multiple_of(head * HD, HD), HD)
        return pltpu.make_async_copy(
            grad_hbm.at[:, columns], grads.at[rows_at(head * HD, HD)], head_sems.at[1, head]
        )

    load_saved.start()
    load_hidden.start()

    barrier = pltpu.get_barrier_semaphore()

    def greet(to_dp, to_ctx):
        pl.semaphore_signal(
            barrier, inc=1, device_id=(to_dp, to_ctx), device_id_type=pl.DeviceIdType.MESH
        )

    greet(above, ctx)
    greet(below, ctx)

    @pl.loop(1, CTX)
    def _(step):
        greet(dp, (ctx + step) % CTX)
        greet(*plane_partner(dp, ctx, step))
        greet(core * Z + z, (ctx + step) % CTX)

    @pl.when(core != x_lo)
    def _():
        greet(*plane_partner(dp, ctx, 0))
        greet(core * Z + z, ctx)

    @pl.loop(0, QH)
    def _(head):
        load_query(head).start()
        load_grad(head).start()

    same = jnp.where(iota((ROWS, ROWS), 0) == iota((ROWS, ROWS), 1), 1.0, 0.0).astype(BF)
    before = jnp.where(iota((ROWS, ROWS), 0) < iota((ROWS, ROWS), 1), 1.0, 0.0).astype(BF)
    route = route_ref[...]
    coming = lax.shift_right_logical(route, 7) == ctx
    rank = jnp.dot(jnp.where(coming, 1.0, 0.0).astype(BF), before, preferred_element_type=F32)
    rank = jnp.where(coming, rank.astype(jnp.int32), -1)
    place = route - ctx * ROWS
    parts = []
    for pack in range(CTX):
        to_rank = one_hot(rank[pack : pack + 1], (CAP, ROWS))
        to_place = one_hot(place[pack : pack + 1], (ROWS, ROWS))
        parts.append(nt_dot(to_rank, to_place).astype(BF))
    owner = jnp.concatenate(parts, axis=0)
    owner_turned[...] = nt_dot(same, owner).astype(BF)
    load_saved.wait()
    for part in range(4):
        columns = slice(part * 1024, (part + 1) * 1024)
        staged[:, columns] = jnp.dot(
            owner, saved_ref[:, columns], preferred_element_type=F32
        ).astype(BF)

    pl.semaphore_wait(barrier, 2 + 3 * (CTX - 1) + jnp.where(core != x_lo, 2, 0))

    shard = whole.at[rows_at((dp * CTX + ctx) * CAP, CAP)]

    def plane_copy(step):
        to_dp, to_ctx = plane_partner(dp, ctx, step)
        return remote(
            weight_ref, shard, plane_sems.at[0, step], plane_sems.at[1, ctx], to_dp, to_ctx
        )

    own_shard = pltpu.make_async_copy(weight_ref, shard, own_sems.at[3])

    @pl.when(core == x_lo)
    def _():
        own_shard.start()

    @pl.when(core != x_lo)
    def _():
        plane_copy(0).start()

    @pl.loop(1, 16)
    def _(step):
        plane_copy(step).start()

    def window(own, whole_window, which):
        sems = [window_sems.at[which, kind] for kind in range(4)]
        return Window(own, whole_window, *sems, own_sems.at[which], dp, ctx)

    keys = window(key_ref, key_window, 0)
    values = window(value_own, value_window, 1)
    keys.start()
    saved_exchange = Exchange(
        staged,
        saved_slots,
        slot_sems.at[0],
        slot_sems.at[1],
        own_sems.at[2],
        dp,
        ctx,
        slice(0, D),
    )
    saved_exchange.start()

    own_owner = lax.shift_right_logical(route_ref[pl.ds(ctx, 1)], 7)
    hit = own_owner == iota((CTX, ROWS), 0)
    count = jnp.dot(jnp.where(hit, 1.0, 0.0).astype(BF), before, preferred_element_type=F32)
    own_rank = jnp.sum(jnp.where(hit, count, 0.0), axis=0, keepdims=True).astype(jnp.int32)
    pack_ref[...] = one_hot(own_owner * CAP + own_rank, (SLOTS, ROWS))
    pack_turned[...] = nt_dot(same, pack_ref[...]).astype(BF)

    empty[...] = jnp.zeros_like(empty)
    for back in range(1, BACK + 1):

        @pl.when(chip < back)
        def _(back=back):
            hole = pl.ds((8 - 2 * back) * ROWS, 2 * ROWS)
            pltpu.sync_copy(empty, key_window.at[hole])
            pltpu.sync_copy(empty, value_window.at[hole])

    @pl.when(core == x_lo)
    def _():
        own_shard.wait()

    @pl.loop(0, CTX)
    def _(source):
        @pl.when(jnp.logical_or(core != x_lo, source != ctx))
        def _():
            shard_in = whole.at[rows_at(((core * Z + z) * CTX + source) * CAP, CAP)]
            remote(
                weight_ref, shard_in, plane_sems.at[0, 0], plane_sems.at[1, source], dp, other
            ).wait_recv()

    half = CHUNK // 2

    def piece(at_core, offset, part):
        start = (at_core * Z + (z + Z + offset) % Z) * CHUNK + part * half
        return whole.at[rows_at(start, half)]

    def up(step, part, offset):
        block = piece(core, offset, part)
        return remote(
            block, block, ring_sems.at[0, step, part], ring_sems.at[1, step, part], above, ctx
        )

    def down(step, part, offset):
        block = piece(core, offset, part)
        return remote(
            block, block, ring_sems.at[2, step, part], ring_sems.at[3, step, part], below, ctx
        )

    def pair(at_core, offset, part):
        block = piece(at_core, offset, part)
        index = offset + 3
        return remote(
            block, block, pair_sems.at[0, index, part], pair_sems.at[1, index, part], dp, other
        )

    for part in range(2):
        up(0, part, 0).start()
        down(0, part, 0).start()
        pair(core, 0, part).start()

    position = ctx * ROWS + iota((1, ROWS), 1)
    doc_start = jnp.zeros((1, ROWS), jnp.int32)
    doc_end = jnp.int32(0)
    for n in range(8):
        length = length_ref[0, n]
        doc_end = doc_end + length
        doc_start = doc_start + jnp.where(position >= doc_end, length, 0)
    left = iota((1, ROWS), 1) < VB

    for block in range(USED // VB):
        column = jnp.maximum(2 * ctx - 16 + block, 0)
        seen = jnp.where(left, visible_ref[2 * ctx, column], visible_ref[2 * ctx + 1, column])
        key_position = ctx * ROWS - 1024 + block * VB + iota((VB, ROWS), 0)
        allowed = (key_position >= doc_start) & (key_position <= position) & (seen == 1)
        bias[block * VB : (block + 1) * VB] = jnp.where(allowed, 0.0, -1e30)

    @pl.loop(0, QH)
    def _(head):
        load_query(head).wait()
        load_grad(head).wait()

    used = pl.ds(pl.multiple_of(core * ROWS, ROWS), USED)
    unused = pl.ds(pl.multiple_of((1 - core) * USED, ROWS), ROWS)
    key_terms[unused] = jnp.zeros((ROWS, KVW), BF)
    value_terms[unused] = jnp.zeros((ROWS, KVW), BF)

    def forward(group):
        columns = slice(group * HD, (group + 1) * HD)
        rows = slice(group * GROUP * HD, (group + 1) * GROUP * HD)

        @pl.loop(0, GROUP // 2)
        def _(two):
            for head in range(2):
                at = pl.multiple_of((group * GROUP + two * 2 + head) * HD, HD)
                scores = nt_dot(key_window[used, columns], queries[pl.ds(at, HD)]) + bias[...]
                top = jnp.max(scores, axis=0, keepdims=True)
                raised = jnp.exp((scores - top) * SCALE)
                weights = raised * (1.0 / jnp.sum(raised, axis=0, keepdims=True))
                weights_all[:, pl.ds(at, HD)] = weights.astype(BF)

        value_terms[used, columns] = jnp.dot(
            weights_all[:, rows], grads[rows], preferred_element_type=F32
        ).astype(BF)

    query_parts = []

    def backward(group):
        columns = slice(group * HD, (group + 1) * HD)
        rows = slice(group * GROUP * HD, (group + 1) * GROUP * HD)

        @pl.loop(0, GROUP // 2)
        def _(two):
            for head in range(2):
                index = group * GROUP + two * 2 + head
                at = pl.multiple_of(index * HD, HD)
                to = pl.multiple_of((two * 2 + head) * HD, HD)
                weights = weights_all[:, pl.ds(at, HD)].astype(F32)
                dweights = nt_dot(value_window[used, columns], grads[pl.ds(at, HD)])
                dscores_all[:, pl.ds(to, HD)] = (
                    (weights * SCALE)
                    * (dweights.astype(BF).astype(F32) - delta[pl.ds(index, 1)])
                ).astype(BF)

        key_terms[used, columns] = jnp.dot(
            dscores_all[...], queries[rows], preferred_element_type=F32
        ).astype(BF)
        keys_turned = nt_dot(same, key_window[used, columns]).astype(BF)
        query_grad = jnp.dot(
            keys_turned, dscores_all[...], preferred_element_type=F32
        ).astype(BF)
        for head in range(GROUP):
            at = (group * GROUP + head) * HD
            staged_grad[:, at : at + HD] = nt_dot(
                pack_ref[...], query_grad[:, head * HD : (head + 1) * HD]
            ).astype(BF)
        part = Exchange(
            staged_grad,
            query_slots,
            query_sems.at[0, group],
            query_sems.at[1, group],
            own_sems.at[4 + group],
            dp,
            ctx,
            rows,
        )
        part.start()
        query_parts.append(part)

    keys.hand_on()
    keys.arrive()
    for step in range(3):
        for part in range(2):
            up(step, part, -step - 1).wait_recv()
            if step < 2 or part == 0:
                up(step + 1, part, -step - 1).start()
            pair(core, -step - 1, part).start()
            down(step, part, step + 1).wait_recv()
            if step < 2 or part == 1:
                down(step + 1, part, step + 1).start()
            pair(core, step + 1, part).start()
        forward(step)
    up(3, 0, 4).wait_recv()
    pair(core, 4, 0).start()
    down(3, 1, 4).wait_recv()
    pair(core, 4, 1).start()
    load_hidden.wait()
    for offset in range(-3, 5):
        for part in range(2):
            pair(1 - core, offset, part).wait_recv()
    value_own[...] = jnp.dot(hidden_ref[...], whole[...], preferred_element_type=F32).astype(BF)
    values.start()
    forward(3)

    def term_sum(which, terms, columns):
        gradient = min(which, 1)
        return Terms(
            terms,
            near_in.at[gradient],
            far_out.at[gradient],
            far_in.at[gradient],
            totals.at[gradient],
            [term_sems.at[which, kind] for kind in range(4)],
            dp,
            ctx,
            columns,
        )

    value_sum = term_sum(0, value_terms, slice(0, KVW))
    key_sums = [
        term_sum(1 + part, key_terms, slice(part * 256, (part + 1) * 256)) for part in range(2)
    ]
    value_sum.start()
    values.hand_on()
    value_sum.send()
    diagonal = jnp.where(iota((CHUNK, CHUNK), 0) == iota((CHUNK, CHUNK), 1), 1.0, 0.0).astype(BF)
    for block in range(D // CHUNK):
        rows = slice(block * CHUNK, (block + 1) * CHUNK)
        turned[rows] = nt_dot(diagonal, hidden_ref[:, rows]).astype(BF)

    saved_exchange.finish()
    ones = jnp.ones((8, HD), BF)

    @pl.loop(0, QH // 4)
    def _(four):
        for head in range(4):
            index = four * 4 + head
            at = pl.ds(pl.multiple_of(index * HD, HD), HD)
            saved = jnp.dot(pack_turned[...], saved_slots[:, at], preferred_element_type=F32)
            product = saved * grads[at].astype(F32)
            high = product.astype(BF)
            low = (product - high.astype(F32)).astype(BF)
            delta[pl.ds(index, 1)] = (nt_dot(ones, high) + nt_dot(ones, low))[:1]

    values.arrive()
    backward(0)
    value_sum.add()
    value_grad[...] = totals[0].astype(BF)

    offsets = (4, 3, -3, 2, -2, 1, -1, 0)

    def partial_at(at_core, offset):
        start = (at_core * Z + (z + Z + offset) % Z) * CHUNK
        return jnp.dot(
            turned[rows_at(start, CHUNK)], value_grad[...], preferred_element_type=F32
        ).astype(BF)

    def pair_back(index):
        return remote(
            theirs.at[index],
            from_pair.at[index],
            pair_back_sems.at[0, index],
            pair_back_sems.at[1, index],
            dp,
            other,
        )

    for index, offset in enumerate(offsets):
        theirs[index] = partial_at(1 - core, offset)
        pair_back(index).start()
    for index, offset in enumerate(offsets):
        mine[index] = partial_at(core, offset)

    def spans(part):
        return slice(part * half, (part + 1) * half)

    def up_back(step, part):
        return remote(
            up_out.at[step, spans(part)],
            up_in.at[step, spans(part)],
            ring_back_sems.at[0, step, part],
            ring_back_sems.at[1, step, part],
            above,
            ctx,
        )

    def down_back(step, part):
        return remote(
            down_out.at[step, spans(part)],
            down_in.at[step, spans(part)],
            ring_back_sems.at[2, step, part],
            ring_back_sems.at[3, step, part],
            below,
            ctx,
        )

    def chip_sum(index, part):
        return mine[index, spans(part)].astype(F32) + from_pair[index, spans(part)].astype(F32)

    pair_back(0).wait_recv()
    up_out[0, spans(0)] = chip_sum(0, 0).astype(BF)
    up_back(0, 0).start()
    down_out[0, spans(1)] = chip_sum(0, 1).astype(BF)
    down_back(0, 1).start()

    def ring_back(step):
        pair_back(2 * step - 1).wait_recv()
        pair_back(2 * step).wait_recv()
        if step == 1:
            up_out[1, spans(1)] = chip_sum(1, 1).astype(BF)
            up_back(1, 1).start()
            down_out[1, spans(0)] = chip_sum(2, 0).astype(BF)
            down_back(1, 0).start()
        for index, ring, out, arrived, kept in (
            (2 * step - 1, up_back, up_out, up_in, 0),
            (2 * step, down_back, down_out, down_in, 1),
        ):
            for part in (kept,) if step == 1 else (1 - kept, kept):
                ring(step - 1, part).wait_recv()
                out[step, spans(part)] = (
                    chip_sum(index, part) + arrived[step - 1, spans(part)].astype(F32)
                ).astype(BF)
                ring(step, part).start()

    backward(1)
    key_sums[0].start()
    ring_back(1)
    key_sums[0].send()
    backward(2)
    ring_back(2)
    backward(3)
    key_sums[1].start()
    ring_back(3)
    key_sums[1].send()
    pair_back(7).wait_recv()
    for part in (0, 1):
        up_back(3, part).wait_recv()
        down_back(3, part).wait_recv()
        mine[7, spans(part)] = (
            chip_sum(7, part)
            + up_in[3, spans(part)].astype(F32)
            + down_in[3, spans(part)].astype(F32)
        ).astype(BF)

    plane = x_lo * 8 + chip

    def plane_back(step):
        to_ctx = (ctx + step) % CTX
        return remote(
            mine.at[7, rows_at(to_ctx * CAP, CAP)],
            plane_in.at[plane],
            plane_back_sems.at[0, step],
            plane_back_sems.at[1, plane],
            core * Z + z,
            to_ctx,
        )

    own_plane = pltpu.make_async_copy(
        mine.at[7, rows_at(ctx * CAP, CAP)], plane_in.at[plane], own_sems.at[3]
    )

    @pl.when(core == x_lo)
    def _():
        own_plane.start()

    @pl.when(core != x_lo)
    def _():
        plane_back(0).start()

    @pl.loop(1, CTX)
    def _(step):
        plane_back(step).start()

    for group in range(KVH):
        columns = slice(group * 1024, (group + 1) * 1024)
        query_parts[group].finish()
        query_grad_ref[:, columns] = jnp.dot(
            owner_turned[...], query_slots[:, columns], preferred_element_type=F32
        ).astype(BF)
    for part in key_sums:
        part.add()
    key_grad_ref[...] = totals[1].astype(BF)

    @pl.when(core == x_lo)
    def _():
        own_plane.wait()

    @pl.loop(0, 16)
    def _(source):
        @pl.when(jnp.logical_or(core != x_lo, source != plane))
        def _():
            remote(
                mine.at[7, pl.ds(0, CAP)],
                plane_in.at[source],
                plane_back_sems.at[0, 0],
                plane_back_sems.at[1, source],
                dp,
                other,
            ).wait_recv()

    weight_sum = plane_in[0].astype(F32)
    for source in range(1, 16):
        weight_sum = weight_sum + plane_in[source].astype(F32)
    weight_grad_ref[...] = weight_sum * (1.0 / math.sqrt(32768.0))

    @pl.when(core != x_lo)
    def _():
        plane_copy(0).wait_send()
        plane_back(0).wait_send()

    @pl.loop(1, 16)
    def _(step):
        plane_copy(step).wait_send()
        plane_back(step).wait_send()

    for step in range(3):
        for part in range(2):
            up(step, part, -step).wait_send()
            down(step, part, step).wait_send()
    up(3, 0, -3).wait_send()
    down(3, 1, 3).wait_send()
    for offset in range(-3, 5):
        for part in range(2):
            pair(core, offset, part).wait_send()
    up_back(0, 0).wait_send()
    down_back(0, 1).wait_send()
    for step in range(1, 4):
        for part in range(2):
            up_back(step, part).wait_send()
            down_back(step, part).wait_send()
    for index in range(8):
        pair_back(index).wait_send()
    keys.finish()
    values.finish()
    for part in [value_sum] + key_sums:
        part.finish()


def local(
    hidden,
    value_weight,
    queries,
    key_rows,
    attn_saved,
    grad_out,
    doc_lengths,
    routing,
    visible_blocks,
):
    vmem = pl.BlockSpec(memory_space=pltpu.VMEM)
    smem = pl.BlockSpec(memory_space=pltpu.SMEM)
    hbm = pl.BlockSpec(memory_space=pltpu.HBM)
    dma = pltpu.SemaphoreType.DMA
    chunk = (CHUNK, KVW)
    blocks = (2, BACK + 1, ROWS, KVW)
    grad_query, grad_key, grad_weight = pl.pallas_call(
        kernel,
        out_shape=(
            jax.ShapeDtypeStruct((ROWS, D), BF),
            jax.ShapeDtypeStruct((ROWS, KVW), BF),
            jax.ShapeDtypeStruct((CAP, KVW), F32),
        ),
        in_specs=[smem, smem, hbm, hbm, hbm, hbm, vmem, hbm, hbm],
        out_specs=(vmem, vmem, vmem),
        scratch_shapes=[
            pltpu.VMEM((ROWS, D), BF),
            pltpu.VMEM((D, ROWS), BF),
            pltpu.VMEM((QH * HD, HD), BF),
            pltpu.VMEM((QH * HD, HD), BF),
            pltpu.VMEM((ROWS, D), BF),
            pltpu.VMEM((SLOTS, D), BF),
            pltpu.VMEM((SLOTS, D), BF),
            pltpu.VMEM((ROWS, SLOTS), BF),
            pltpu.VMEM((SLOTS, ROWS), BF),
            pltpu.VMEM((ROWS, SLOTS), BF),
            pltpu.VMEM((USED, ROWS), F32),
            pltpu.VMEM((QH, ROWS), F32),
            pltpu.VMEM((D, KVW), BF),
            pltpu.VMEM((ROWS, KVW), BF),
            pltpu.VMEM((2 * ROWS, KVW), BF),
            pltpu.VMEM((WIN, KVW), BF),
            pltpu.VMEM((WIN, KVW), BF),
            pltpu.VMEM((USED, QH * HD), BF),
            pltpu.VMEM((USED, GROUP * HD), BF),
            pltpu.VMEM((WIN, KVW), BF),
            pltpu.VMEM((WIN, KVW), BF),
            pltpu.VMEM((SLOTS, D), BF),
            pltpu.VMEM((SLOTS, D), BF),
            pltpu.VMEM(blocks, BF),
            pltpu.VMEM(blocks, BF),
            pltpu.VMEM(blocks, BF),
            pltpu.VMEM((2, ROWS, KVW), F32),
            pltpu.VMEM((ROWS, KVW), BF),
            pltpu.VMEM((8,) + chunk, BF),
            pltpu.VMEM((8,) + chunk, BF),
            pltpu.VMEM((8,) + chunk, BF),
            pltpu.VMEM((4,) + chunk, BF),
            pltpu.VMEM((4,) + chunk, BF),
            pltpu.VMEM((4,) + chunk, BF),
            pltpu.VMEM((4,) + chunk, BF),
            pltpu.VMEM((16, CAP, KVW), BF),
            dma((2,)),
            dma((2, QH)),
            dma((8,)),
            dma((2, 16)),
            dma((4, 4, 2)),
            dma((2, 8, 2)),
            dma((2, 4, BACK + 1)),
            dma((2, CTX)),
            dma((3, 4, BACK + 1)),
            dma((2, KVH, CTX)),
            dma((2, 8)),
            dma((4, 4, 2)),
            dma((2, 16)),
        ],
        compiler_params=pltpu.CompilerParams(
            has_side_effects=True, vmem_limit_bytes=60 * 1024 * 1024, collective_id=0
        ),
        name="attention_backward",
    )(
        doc_lengths,
        visible_blocks[0],
        value_weight,
        hidden[0],
        key_rows[0],
        attn_saved[0],
        routing.reshape(CTX, ROWS),
        queries[0],
        grad_out[0],
    )
    return (grad_query[None], grad_key[None], grad_weight)


def solution(mesh):
    return jax.shard_map(
        local,
        mesh=mesh,
        in_specs=(
            P("dp", "ctx", None),
            P(("dp", "ctx"), None),
            P("dp", "ctx", None),
            P("dp", "ctx", None),
            P("dp", "ctx", None),
            P("dp", "ctx", None),
            P("dp", None),
            P("dp", None),
            P("dp", None, None),
        ),
        out_specs=(P("dp", "ctx", None), P("dp", "ctx", None), P(("dp", "ctx"), None)),
        check_vma=False,
    )
```

time: 2090 us -> 129 us (0.06)
  the two profiles are of different devices: /device:TPU:128 before, /device:TPU:1 now
where the time goes in v2:
time: 129 us; the launch traced here: 128 us
  Pallas kernels  123 us (95%)
  local copies, waits for them, and re-layouts  3.7 us (3%)
    pallas_call x1, Pallas kernels, local(): pl.pallas_call(kernel, out_shape=(jax.ShapeDtypeStruct((ROWS, D), BF), ja...  123 us
    unnamed x7, local copies, waits for them, and re-layouts  3.7 us

profile of v2, /device:TPU:1, one launch (start us, length us, event | category | flops | bytes accessed | tf_op | source)
XLA Modules:
  0.0 127.8 jit_solution(11392395159325960099)
XLA Ops:
  0.6 123.5 %attention_backward.1 = (bf16[128,4096]{1,0:T(8,128)(2,1)}, bf16[128,512]{1,0:T(8,128)(2,1)}, f32[16,512]{1,0:T(8,128)}) custom-call(s32[1,8]{1,0:T(1,128)} %length_ref.1, s32[32,32]{1,0:T(8,128)} %bitcast.16, bf16[16,512]{1,0:T(8,128)(2,1)} %weight_ref.1, bf16[128,4096]{1,0:T(8,128)(2,1)} %bitcast.9, bf16[128,512]{1,0:T(8,128)(2,1)} %bitcast.14, ...), custom_call_target="tpu_custom_call" | custom-call | tf_op jit(solution)/shard_map/attention_backward/pallas_call | solution.py:856
  124.1 0.0 copy-start
  124.1 2.3 %copy.15 = bf16[1,128,4096]{2,1,0:T(8,128)(2,1)} copy(bf16[1,128,4096]{2,1,0:T(8,128)(2,1)} %bitcast.13) | data formatting | bytes 2097152
  126.5 0.0 copy-done
  126.5 0.0 copy-start.1
  126.5 0.7 copy.16
  127.1 0.1 copy-done.1
  127.2 0.6 copy.17
Async XLA Ops:
  124.1 2.3 %copy-start = (bf16[128,512]{1,0:T(8,128)(2,1)S(1)}, bf16[128,512]{1,0:T(8,128)(2,1)}, u32[]{:S(2)}) copy-start(bf16[128,512]{1,0:T(8,128)(2,1)} %get-tuple-element.7) | copy-start | bytes 393220
  126.5 0.8 copy-start.1

commit v3 on v2

--- a/solution.py
+++ b/solution.py
@@ -428,7 +428,6 @@
         ctx,
         slice(0, D),
     )
-    saved_exchange.start()
 
     own_owner = lax.shift_right_logical(route_ref[pl.ds(ctx, 1)], 7)
     hit = own_owner == iota((CTX, ROWS), 0)
@@ -577,9 +576,7 @@
         part.start()
         query_parts.append(part)
 
-    keys.hand_on()
-    keys.arrive()
-    for step in range(3):
+    def ring(step):
         for part in range(2):
             up(step, part, -step - 1).wait_recv()
             if step < 2 or part == 0:
@@ -589,17 +586,16 @@
             if step < 2 or part == 1:
                 down(step + 1, part, step + 1).start()
             pair(core, step + 1, part).start()
-        forward(step)
-    up(3, 0, 4).wait_recv()
-    pair(core, 4, 0).start()
-    down(3, 1, 4).wait_recv()
-    pair(core, 4, 1).start()
-    load_hidden.wait()
-    for offset in range(-3, 5):
-        for part in range(2):
-            pair(1 - core, offset, part).wait_recv()
-    value_own[...] = jnp.dot(hidden_ref[...], whole[...], preferred_element_type=F32).astype(BF)
-    values.start()
+
+    keys.hand_on()
+    ring(0)
+    keys.arrive()
+    saved_exchange.start()
+    forward(0)
+    ring(1)
+    forward(1)
+    ring(2)
+    forward(2)
     forward(3)
 
     def term_sum(which, terms, columns):
@@ -621,7 +617,16 @@
         term_sum(1 + part, key_terms, slice(part * 256, (part + 1) * 256)) for part in range(2)
     ]
     value_sum.start()
-    values.hand_on()
+    up(3, 0, 4).wait_recv()
+    pair(core, 4, 0).start()
+    down(3, 1, 4).wait_recv()
+    pair(core, 4, 1).start()
+    load_hidden.wait()
+    for offset in range(-3, 5):
+        for part in range(2):
+            pair(1 - core, offset, part).wait_recv()
+    value_own[...] = jnp.dot(hidden_ref[...], whole[...], preferred_element_type=F32).astype(BF)
+    values.start()
     value_sum.send()
     diagonal = jnp.where(iota((CHUNK, CHUNK), 0) == iota((CHUNK, CHUNK), 1), 1.0, 0.0).astype(BF)
     for block in range(D // CHUNK):
@@ -642,8 +647,7 @@
             low = (product - high.astype(F32)).astype(BF)
             delta[pl.ds(index, 1)] = (nt_dot(ones, high) + nt_dot(ones, low))[:1]
 
-    values.arrive()
-    backward(0)
+    values.hand_on()
     value_sum.add()
     value_grad[...] = totals[0].astype(BF)
 
@@ -722,16 +726,17 @@
                 ).astype(BF)
                 ring(step, part).start()
 
+    values.arrive()
+    backward(0)
+    ring_back(1)
     backward(1)
     key_sums[0].start()
-    ring_back(1)
+    ring_back(2)
     key_sums[0].send()
     backward(2)
-    ring_back(2)
+    ring_back(3)
     backward(3)
     key_sums[1].start()
-    ring_back(3)
-    key_sums[1].send()
     pair_back(7).wait_recv()
     for part in (0, 1):
         up_back(3, part).wait_recv()
@@ -771,6 +776,7 @@
     def _(step):
         plane_back(step).start()
 
+    key_sums[1].send()
     for group in range(KVH):
         columns = slice(group * 1024, (group + 1) * 1024)
         query_parts[group].finish()

time: 129 us -> 130 us (level)
  Pallas kernels: 123 us -> 125 us
    pallas_call x1, Pallas kernels: 123 us -> 125 us  [local(): pl.pallas_call(kernel, out_shape=(jax.ShapeDtypeStruct((ROWS, D), BF), ja...]
where the time goes in v3:
time: 130 us
  Pallas kernels  125 us (96%)
  local copies, waits for them, and re-layouts  3.7 us (3%)
    pallas_call x1, Pallas kernels, local(): pl.pallas_call(kernel, out_shape=(jax.ShapeDtypeStruct((ROWS, D), BF), ja...  125 us
    unnamed x7, local copies, waits for them, and re-layouts  3.7 us

profile of v3, /device:TPU:1, one launch (start us, length us, event | category | flops | bytes accessed | tf_op | source)
XLA Modules:
  0.0 129.6 jit_solution(14393648275140476659)
XLA Ops:
  0.6 125.3 %attention_backward.1 = (bf16[128,4096]{1,0:T(8,128)(2,1)}, bf16[128,512]{1,0:T(8,128)(2,1)}, f32[16,512]{1,0:T(8,128)}) custom-call(s32[1,8]{1,0:T(1,128)} %length_ref.1, s32[32,32]{1,0:T(8,128)} %bitcast.16, bf16[16,512]{1,0:T(8,128)(2,1)} %weight_ref.1, bf16[128,4096]{1,0:T(8,128)(2,1)} %bitcast.9, bf16[128,512]{1,0:T(8,128)(2,1)} %bitcast.14, ...), custom_call_target="tpu_custom_call" | custom-call | tf_op jit(solution)/shard_map/attention_backward/pallas_call | solution.py:862
  125.9 0.0 copy-start
  125.9 2.3 %copy.15 = bf16[1,128,4096]{2,1,0:T(8,128)(2,1)} copy(bf16[1,128,4096]{2,1,0:T(8,128)(2,1)} %bitcast.13) | data formatting | bytes 2097152
  128.3 0.0 copy-done
  128.3 0.0 copy-start.1
  128.3 0.7 copy.16
  128.9 0.1 copy-done.1
  129.0 0.6 copy.17
Async XLA Ops:
  125.9 2.3 %copy-start = (bf16[128,512]{1,0:T(8,128)(2,1)S(1)}, bf16[128,512]{1,0:T(8,128)(2,1)}, u32[]{:S(2)}) copy-start(bf16[128,512]{1,0:T(8,128)(2,1)} %get-tuple-element.7) | copy-start | bytes 393220
  128.3 0.8 copy-start.1

commit v4 on v3

v4 whole, which is shorter than its diff:
```python
import math

import jax
import jax.numpy as jnp
from jax import lax
from jax.experimental import pallas as pl
from jax.experimental.pallas import tpu as pltpu
from jax.sharding import PartitionSpec as P

QH = 32
HD = 128
VB = 64
ROWS = 128
CTX = 16
CAP = 16
TOKENS = 2048
PAIR = 2 * HD
KVH = 4
Z = 8
D = 4096
KVW = 512
USED = 1152
CHUNK = 256
BF = jnp.bfloat16
F32 = jnp.float32
NT = (((1,), (1,)), ((), ()))
TN = (((0,), (0,)), ((), ()))
SCALE = 1.0 / math.sqrt(HD)


def remote(source, target, send_sem, recv_sem, dp, ctx):
    return pltpu.make_async_remote_copy(
        src_ref=source,
        dst_ref=target,
        send_sem=send_sem,
        recv_sem=recv_sem,
        device_id=(dp, ctx),
        device_id_type=pl.DeviceIdType.MESH,
    )


def rows_at(start, size):
    return pl.ds(pl.multiple_of(start, size), size)


def iota(shape, axis):
    return lax.broadcasted_iota(jnp.int32, shape, axis)


def nt_dot(first, second):
    return lax.dot_general(first, second, NT, preferred_element_type=F32)


def tn_dot(first, second):
    return lax.dot_general(first, second, TN, preferred_element_type=F32)


class Exchange:
    def __init__(self, source, target, sems, own_sem, dp, ctx):
        self.source, self.target = source, target
        self.sems, self.own_sem, self.dp, self.ctx = sems, own_sem, dp, ctx

    def copy(self, step):
        partner = (self.ctx + step) % CTX
        return remote(
            self.source(partner),
            self.target,
            self.sems.at[0, step],
            self.sems.at[1, step],
            self.dp,
            partner,
        )

    def own_copy(self):
        return pltpu.make_async_copy(self.source(self.ctx), self.target, self.own_sem)

    def start(self):
        self.own_copy().start()

        @pl.loop(1, CTX)
        def _(step):
            self.copy(step).start()

    def arrive(self):
        self.own_copy().wait()

        @pl.loop(1, CTX)
        def _(step):
            self.copy(step).wait_recv()

    def finish(self):
        @pl.loop(1, CTX)
        def _(step):
            self.copy(step).wait_send()


def plane_partner(dp, ctx, step):
    chip = ((dp // Z) * 8 + ctx // 2 + step) % 16
    return (chip // 8) * Z + dp % Z, (chip % 8) * 2 + dp // Z


def kernel(
    length_ref,
    visible_ref,
    weight_ref,
    hidden_hbm,
    key_hbm,
    saved_hbm,
    route_ref,
    query_hbm,
    grad_hbm,
    query_grad_ref,
    key_grad_ref,
    weight_grad_ref,
    hidden_ref,
    turned,
    queries,
    grads,
    saved,
    keys,
    keys_turned,
    values,
    to_owner,
    bias,
    delta,
    whole,
    value_own,
    weights_all,
    key_terms,
    value_terms,
    key_rounded,
    value_rounded,
    query_rows,
    query_owned,
    key_in,
    value_in,
    value_grad,
    mine,
    theirs,
    from_pair,
    up_in,
    down_in,
    up_out,
    down_out,
    plane_in,
    load_sem,
    own_sems,
    plane_sems,
    ring_sems,
    pair_sems,
    exchange_sems,
    pair_back_sems,
    ring_back_sems,
    plane_back_sems,
):
    dp, ctx = lax.axis_index("dp"), lax.axis_index("ctx")
    x_lo, z = dp // Z, dp % Z
    chip, core = ctx // 2, ctx % 2
    other = ctx + 1 - 2 * core
    above, below = x_lo * Z + (z + 1) % Z, x_lo * Z + (z + Z - 1) % Z

    load_hidden = pltpu.make_async_copy(hidden_hbm, hidden_ref, load_sem)
    load_hidden.start()

    barrier = pltpu.get_barrier_semaphore()

    def greet(to_dp, to_ctx):
        pl.semaphore_signal(
            barrier, inc=1, device_id=(to_dp, to_ctx), device_id_type=pl.DeviceIdType.MESH
        )

    greet(above, ctx)
    greet(below, ctx)

    @pl.loop(1, CTX)
    def _(step):
        greet(dp, (ctx + step) % CTX)
        greet(*plane_partner(dp, ctx, step))
        greet(core * Z + z, (ctx + step) % CTX)

    @pl.when(core != x_lo)
    def _():
        greet(*plane_partner(dp, ctx, 0))
        greet(core * Z + z, ctx)

    same = jnp.where(iota((ROWS, ROWS), 0) == iota((ROWS, ROWS), 1), 1.0, 0.0).astype(BF)
    diagonal = jnp.where(iota((CHUNK, CHUNK), 0) == iota((CHUNK, CHUNK), 1), 1.0, 0.0).astype(BF)
    left = iota((1, ROWS), 1) < VB

    @pl.loop(0, CTX)
    def _(block):
        to_owner[:, rows_at(block * ROWS, ROWS)] = jnp.where(
            route_ref[pl.ds(block, 1)] == iota((TOKENS, ROWS), 0), 1.0, 0.0
        ).astype(BF)

    key_terms[...] = jnp.zeros_like(key_terms)
    value_terms[...] = jnp.zeros_like(value_terms)
    pl.semaphore_wait(barrier, 2 + 3 * (CTX - 1) + jnp.where(core != x_lo, 2, 0))

    shard = whole.at[rows_at((dp * CTX + ctx) * CAP, CAP)]

    def plane_copy(step):
        to_dp, to_ctx = plane_partner(dp, ctx, step)
        return remote(
            weight_ref, shard, plane_sems.at[0, step], plane_sems.at[1, ctx], to_dp, to_ctx
        )

    own_shard = pltpu.make_async_copy(weight_ref, shard, own_sems.at[3])

    @pl.when(core == x_lo)
    def _():
        own_shard.start()

    @pl.when(core != x_lo)
    def _():
        plane_copy(0).start()

    @pl.loop(1, 16)
    def _(step):
        plane_copy(step).start()

    def wide(index, width):
        return pl.ds(pl.multiple_of(index * width, width), width)

    here = rows_at(ctx * ROWS, ROWS)

    def exchange(which, source, target):
        return Exchange(source, target, exchange_sems.at[which], own_sems.at[4 + which], dp, ctx)

    key_move = exchange(0, lambda to: key_hbm.at[:, wide(to // 4, HD)], keys.at[here])
    query_move = exchange(1, lambda to: query_hbm.at[:, wide(to, PAIR)], queries.at[here])
    grad_move = exchange(2, lambda to: grad_hbm.at[:, wide(to, PAIR)], grads.at[here])
    saved_move = exchange(3, lambda to: saved_hbm.at[:, wide(to, PAIR)], saved.at[here])
    value_move = exchange(4, lambda to: value_own.at[:, wide(to // 4, HD)], values.at[here])
    value_back = exchange(5, lambda to: value_rounded.at[rows_at(to * ROWS, ROWS)], value_in.at[ctx])
    key_back = exchange(6, lambda to: key_rounded.at[rows_at(to * ROWS, ROWS)], key_in.at[ctx])
    query_back = exchange(
        7, lambda to: query_owned.at[rows_at(to * ROWS, ROWS)], query_grad_ref.at[:, wide(ctx, PAIR)]
    )
    key_move.start()
    query_move.start()

    @pl.when(core == x_lo)
    def _():
        own_shard.wait()

    @pl.loop(0, CTX)
    def _(source):
        @pl.when(jnp.logical_or(core != x_lo, source != ctx))
        def _():
            shard_in = whole.at[rows_at(((core * Z + z) * CTX + source) * CAP, CAP)]
            remote(
                weight_ref, shard_in, plane_sems.at[0, 0], plane_sems.at[1, source], dp, other
            ).wait_recv()

    half = CHUNK // 2

    def piece(at_core, offset, part):
        start = (at_core * Z + (z + Z + offset) % Z) * CHUNK + part * half
        return whole.at[rows_at(start, half)]

    def up(step, part, offset):
        block = piece(core, offset, part)
        return remote(
            block, block, ring_sems.at[0, step, part], ring_sems.at[1, step, part], above, ctx
        )

    def down(step, part, offset):
        block = piece(core, offset, part)
        return remote(
            block, block, ring_sems.at[2, step, part], ring_sems.at[3, step, part], below, ctx
        )

    def pair(at_core, offset, part):
        block = piece(at_core, offset, part)
        index = offset + 3
        return remote(
            block, block, pair_sems.at[0, index, part], pair_sems.at[1, index, part], dp, other
        )

    for part in range(2):
        up(0, part, 0).start()
        down(0, part, 0).start()
        pair(core, 0, part).start()

    def ring(step):
        for part in range(2):
            up(step, part, -step - 1).wait_recv()
            if step < 2 or part == 0:
                up(step + 1, part, -step - 1).start()
            pair(core, -step - 1, part).start()
            down(step, part, step + 1).wait_recv()
            if step < 2 or part == 1:
                down(step + 1, part, step + 1).start()
            pair(core, step + 1, part).start()

    quarters = ((0, 512), (4, 1024), (8, USED), (12, USED))

    def first_block(quarter, block):
        return block - 8 if quarter >= 2 else jnp.int32(0)

    def stacked(pairs, block):
        rows = rows_at(block * ROWS, ROWS)
        return jnp.concatenate([pairs[rows, :HD], pairs[rows, HD:]], axis=0)

    def forward(quarter):
        first, size = quarters[quarter]

        @pl.loop(first, first + 4)
        def _(block):
            base = first_block(quarter, block)
            position = block * ROWS + iota((1, ROWS), 1)
            doc_start = jnp.zeros((1, ROWS), jnp.int32)
            doc_end = jnp.int32(0)
            for n in range(8):
                length = length_ref[0, n]
                doc_end = doc_end + length
                doc_start = doc_start + jnp.where(position >= doc_end, length, 0)
            for part in range(size // VB):
                column = 2 * base + part
                seen = jnp.where(
                    left, visible_ref[2 * block, column], visible_ref[2 * block + 1, column]
                )
                key_position = column * VB + iota((VB, ROWS), 0)
                allowed = (
                    (key_position >= doc_start) & (key_position <= position) & (seen == 1)
                )
                bias[part * VB : (part + 1) * VB] = jnp.where(allowed, 0.0, -1e30)
            window = pl.ds(pl.multiple_of(base * ROWS, ROWS), size)
            scores = nt_dot(keys[window], stacked(queries, block))
            scores = scores + jnp.concatenate([bias[:size], bias[:size]], axis=1)
            top = jnp.max(scores, axis=0, keepdims=True)
            raised = jnp.exp((scores - top) * SCALE)
            weights = raised * (1.0 / jnp.sum(raised, axis=0, keepdims=True))
            weights_all[pl.ds(pl.multiple_of(block * USED, ROWS), size)] = weights.astype(BF)

    def value_part(quarter):
        first, size = quarters[quarter]

        @pl.loop(first, first + 4)
        def _(block):
            window = pl.ds(pl.multiple_of(first_block(quarter, block) * ROWS, ROWS), size)
            stored = pl.ds(pl.multiple_of(block * USED, ROWS), size)
            value_terms[window] += jnp.dot(
                weights_all[stored], stacked(grads, block), preferred_element_type=F32
            )

    def backward(quarter):
        first, size = quarters[quarter]

        @pl.loop(first, first + 4)
        def _(block):
            window = pl.ds(pl.multiple_of(first_block(quarter, block) * ROWS, ROWS), size)
            stored = pl.ds(pl.multiple_of(block * USED, ROWS), size)
            rows = rows_at(block * ROWS, ROWS)
            weights = weights_all[stored].astype(F32)
            dweights = nt_dot(values[window], stacked(grads, block))
            row_delta = jnp.concatenate([delta[:1, rows], delta[1:, rows]], axis=1)
            dscores = (
                (weights * SCALE) * (dweights.astype(BF).astype(F32) - row_delta)
            ).astype(BF)
            key_terms[window] += jnp.dot(
                dscores, stacked(queries, block), preferred_element_type=F32
            )
            query_turned = jnp.dot(
                keys_turned[:, window], dscores, preferred_element_type=F32
            ).astype(BF)
            for head in range(2):
                columns = slice(head * HD, (head + 1) * HD)
                query_rows[rows, columns] = nt_dot(same, query_turned[:, columns]).astype(BF)

    def own_rows():
        @pl.loop(0, TOKENS // CHUNK)
        def _(block):
            rows = rows_at(block * CHUNK, CHUNK)
            query_owned[rows] = jnp.dot(
                to_owner[rows], query_rows[...], preferred_element_type=F32
            ).astype(BF)

        query_back.start()

    key_move.arrive()
    keys_turned[...] = nt_dot(same, keys[...]).astype(BF)
    ring(0)
    ring(1)
    grad_move.start()
    query_move.arrive()
    forward(0)
    ring(2)
    load_hidden.wait()
    forward(1)
    forward(2)
    up(3, 0, 4).wait_recv()
    pair(core, 4, 0).start()
    down(3, 1, 4).wait_recv()
    pair(core, 4, 1).start()
    for offset in range(-3, 5):
        for part in range(2):
            pair(1 - core, offset, part).wait_recv()
    value_own[...] = jnp.dot(hidden_ref[...], whole[...], preferred_element_type=F32).astype(BF)
    value_move.start()
    forward(3)
    grad_move.arrive()
    for quarter in range(4):
        value_part(quarter)
    value_rounded[...] = value_terms[...].astype(BF)
    value_back.start()
    saved_move.start()
    for block in range(D // CHUNK):
        rows = slice(block * CHUNK, (block + 1) * CHUNK)
        turned[rows] = nt_dot(diagonal, hidden_ref[:, rows]).astype(BF)

    def four(arrived, group):
        total = arrived[4 * group].astype(F32)
        for part in range(1, 4):
            total = total + arrived[4 * group + part].astype(F32)
        return total.astype(BF)

    value_back.arrive()
    for group in range(KVH):
        value_grad[:, group * HD : (group + 1) * HD] = four(value_in, group)

    offsets = (4, 3, -3, 2, -2, 1, -1, 0)

    def partial_at(at_core, offset):
        start = (at_core * Z + (z + Z + offset) % Z) * CHUNK
        return jnp.dot(
            turned[rows_at(start, CHUNK)], value_grad[...], preferred_element_type=F32
        ).astype(BF)

    def pair_back(index):
        return remote(
            theirs.at[index],
            from_pair.at[index],
            pair_back_sems.at[0, index],
            pair_back_sems.at[1, index],
            dp,
            other,
        )

    for index, offset in enumerate(offsets):
        theirs[index] = partial_at(1 - core, offset)
        pair_back(index).start()
    for index, offset in enumerate(offsets):
        mine[index] = partial_at(core, offset)

    def spans(part):
        return slice(part * half, (part + 1) * half)

    def up_back(step, part):
        return remote(
            up_out.at[step, spans(part)],
            up_in.at[step, spans(part)],
            ring_back_sems.at[0, step, part],
            ring_back_sems.at[1, step, part],
            above,
            ctx,
        )

    def down_back(step, part):
        return remote(
            down_out.at[step, spans(part)],
            down_in.at[step, spans(part)],
            ring_back_sems.at[2, step, part],
            ring_back_sems.at[3, step, part],
            below,
            ctx,
        )

    def chip_sum(index, part):
        return mine[index, spans(part)].astype(F32) + from_pair[index, spans(part)].astype(F32)

    pair_back(0).wait_recv()
    up_out[0, spans(0)] = chip_sum(0, 0).astype(BF)
    up_back(0, 0).start()
    down_out[0, spans(1)] = chip_sum(0, 1).astype(BF)
    down_back(0, 1).start()

    def ring_back(step):
        pair_back(2 * step - 1).wait_recv()
        pair_back(2 * step).wait_recv()
        if step == 1:
            up_out[1, spans(1)] = chip_sum(1, 1).astype(BF)
            up_back(1, 1).start()
            down_out[1, spans(0)] = chip_sum(2, 0).astype(BF)
            down_back(1, 0).start()
        for index, ring, out, arrived, kept in (
            (2 * step - 1, up_back, up_out, up_in, 0),
            (2 * step, down_back, down_out, down_in, 1),
        ):
            for part in (kept,) if step == 1 else (1 - kept, kept):
                ring(step - 1, part).wait_recv()
                out[step, spans(part)] = (
                    chip_sum(index, part) + arrived[step - 1, spans(part)].astype(F32)
                ).astype(BF)
                ring(step, part).start()

    saved_move.arrive()
    saved_turned = nt_dot(diagonal, saved[...]).astype(BF)

    @pl.loop(0, TOKENS // CHUNK)
    def _(block):
        rows = rows_at(block * CHUNK, CHUNK)
        product = jnp.dot(
            saved_turned, to_owner[:, rows], preferred_element_type=F32
        ) * nt_dot(diagonal, grads[rows])
        for head in range(2):
            delta[head : head + 1, rows] = jnp.sum(
                product[head * HD : (head + 1) * HD], axis=0, keepdims=True
            )

    ring_back(1)
    value_move.arrive()
    backward(0)
    backward(1)
    ring_back(2)
    backward(2)
    backward(3)
    key_rounded[...] = key_terms[...].astype(BF)
    key_back.start()
    ring_back(3)
    own_rows()
    pair_back(7).wait_recv()
    for part in (0, 1):
        up_back(3, part).wait_recv()
        down_back(3, part).wait_recv()
        mine[7, spans(part)] = (
            chip_sum(7, part)
            + up_in[3, spans(part)].astype(F32)
            + down_in[3, spans(part)].astype(F32)
        ).astype(BF)

    plane = x_lo * 8 + chip

    def plane_back(step):
        to_ctx = (ctx + step) % CTX
        return remote(
            mine.at[7, rows_at(to_ctx * CAP, CAP)],
            plane_in.at[plane],
            plane_back_sems.at[0, step],
            plane_back_sems.at[1, plane],
            core * Z + z,
            to_ctx,
        )

    own_plane = pltpu.make_async_copy(
        mine.at[7, rows_at(ctx * CAP, CAP)], plane_in.at[plane], own_sems.at[3]
    )

    @pl.when(core == x_lo)
    def _():
        own_plane.start()

    @pl.when(core != x_lo)
    def _():
        plane_back(0).start()

    @pl.loop(1, CTX)
    def _(step):
        plane_back(step).start()

    key_back.arrive()
    for group in range(KVH):
        key_grad_ref[:, group * HD : (group + 1) * HD] = four(key_in, group)

    @pl.when(core == x_lo)
    def _():
        own_plane.wait()

    @pl.loop(0, 16)
    def _(source):
        @pl.when(jnp.logical_or(core != x_lo, source != plane))
        def _():
            remote(
                mine.at[7, pl.ds(0, CAP)],
                plane_in.at[source],
                plane_back_sems.at[0, 0],
                plane_back_sems.at[1, source],
                dp,
                other,
            ).wait_recv()

    weight_sum = plane_in[0].astype(F32)
    for source in range(1, 16):
        weight_sum = weight_sum + plane_in[source].astype(F32)
    weight_grad_ref[...] = weight_sum * (1.0 / math.sqrt(32768.0))

    @pl.when(core != x_lo)
    def _():
        plane_copy(0).wait_send()
        plane_back(0).wait_send()

    @pl.loop(1, 16)
    def _(step):
        plane_copy(step).wait_send()
        plane_back(step).wait_send()

    for step in range(3):
        for part in range(2):
            up(step, part, -step).wait_send()
            down(step, part, step).wait_send()
    up(3, 0, -3).wait_send()
    down(3, 1, 3).wait_send()
    for offset in range(-3, 5):
        for part in range(2):
            pair(core, offset, part).wait_send()
    up_back(0, 0).wait_send()
    down_back(0, 1).wait_send()
    for step in range(1, 4):
        for part in range(2):
            up_back(step, part).wait_send()
            down_back(step, part).wait_send()
    for index in range(8):
        pair_back(index).wait_send()
    query_back.arrive()
    for part in (
        key_move,
        query_move,
        grad_move,
        saved_move,
        value_move,
        value_back,
        key_back,
        query_back,
    ):
        part.finish()


def local(
    hidden,
    value_weight,
    queries,
    key_rows,
    attn_saved,
    grad_out,
    doc_lengths,
    routing,
    visible_blocks,
):
    vmem = pl.BlockSpec(memory_space=pltpu.VMEM)
    smem = pl.BlockSpec(memory_space=pltpu.SMEM)
    hbm = pl.BlockSpec(memory_space=pltpu.HBM)
    dma = pltpu.SemaphoreType.DMA
    chunk = (CHUNK, KVW)
    grad_query, grad_key, grad_weight = pl.pallas_call(
        kernel,
        out_shape=(
            jax.ShapeDtypeStruct((ROWS, D), BF),
            jax.ShapeDtypeStruct((ROWS, KVW), BF),
            jax.ShapeDtypeStruct((CAP, KVW), F32),
        ),
        in_specs=[smem, smem, hbm, hbm, hbm, hbm, vmem, hbm, hbm],
        out_specs=(vmem, vmem, vmem),
        scratch_shapes=[
            pltpu.VMEM((ROWS, D), BF),
            pltpu.VMEM((D, ROWS), BF),
            pltpu.VMEM((TOKENS, PAIR), BF),
            pltpu.VMEM((TOKENS, PAIR), BF),
            pltpu.VMEM((TOKENS, PAIR), BF),
            pltpu.VMEM((TOKENS, HD), BF),
            pltpu.VMEM((HD, TOKENS), BF),
            pltpu.VMEM((TOKENS, HD), BF),
            pltpu.VMEM((TOKENS, TOKENS), BF),
            pltpu.VMEM((USED, ROWS), F32),
            pltpu.VMEM((2, TOKENS), F32),
            pltpu.VMEM((D, KVW), BF),
            pltpu.VMEM((ROWS, KVW), BF),
            pltpu.VMEM((CTX * USED, PAIR), BF),
            pltpu.VMEM((TOKENS, HD), F32),
            pltpu.VMEM((TOKENS, HD), F32),
            pltpu.VMEM((TOKENS, HD), BF),
            pltpu.VMEM((TOKENS, HD), BF),
            pltpu.VMEM((TOKENS, PAIR), BF),
            pltpu.VMEM((TOKENS, PAIR), BF),
            pltpu.VMEM((CTX, ROWS, HD), BF),
            pltpu.VMEM((CTX, ROWS, HD), BF),
            pltpu.VMEM((ROWS, KVW), BF),
            pltpu.VMEM((8,) + chunk, BF),
            pltpu.VMEM((8,) + chunk, BF),
            pltpu.VMEM((8,) + chunk, BF),
            pltpu.VMEM((4,) + chunk, BF),
            pltpu.VMEM((4,) + chunk, BF),
            pltpu.VMEM((4,) + chunk, BF),
            pltpu.VMEM((4,) + chunk, BF),
            pltpu.VMEM((16, CAP, KVW), BF),
            dma,
            dma((12,)),
            dma((2, 16)),
            dma((4, 4, 2)),
            dma((2, 8, 2)),
            dma((8, 2, CTX)),
            dma((2, 8)),
            dma((4, 4, 2)),
            dma((2, 16)),
        ],
        compiler_params=pltpu.CompilerParams(
            has_side_effects=True, vmem_limit_bytes=60 * 1024 * 1024, collective_id=0
        ),
        name="attention_backward",
    )(
        doc_lengths,
        visible_blocks[0],
        value_weight,
        hidden[0],
        key_rows[0],
        attn_saved[0],
        routing.reshape(CTX, ROWS),
        queries[0],
        grad_out[0],
    )
    return (grad_query[None], grad_key[None], grad_weight)


def solution(mesh):
    return jax.shard_map(
        local,
        mesh=mesh,
        in_specs=(
            P("dp", "ctx", None),
            P(("dp", "ctx"), None),
            P("dp", "ctx", None),
            P("dp", "ctx", None),
            P("dp", "ctx", None),
            P("dp", "ctx", None),
            P("dp", None),
            P("dp", None),
            P("dp", None, None),
        ),
        out_specs=(P("dp", "ctx", None), P("dp", "ctx", None), P(("dp", "ctx"), None)),
        check_vma=False,
    )
```

time: 130 us -> 130 us (level); the launches traced: 130 us -> 128 us
    pallas_call x1, Pallas kernels: 125 us -> 124 us  [local(): pl.pallas_call(kernel, out_shape=(jax.ShapeDtypeStruct((ROWS, D), BF), ja...]
where the time goes in v4:
time: 130 us; the launch traced here: 128 us
  Pallas kernels  124 us (95%)
  local copies, waits for them, and re-layouts  3.7 us (3%)
    pallas_call x1, Pallas kernels, local(): pl.pallas_call(kernel, out_shape=(jax.ShapeDtypeStruct((ROWS, D), BF), ja...  124 us
    unnamed x7, local copies, waits for them, and re-layouts  3.7 us

profile of v4, /device:TPU:1, one launch (start us, length us, event | category | flops | bytes accessed | tf_op | source)
XLA Modules:
  0.0 128.1 jit_solution(1229605349653765301)
XLA Ops:
  0.6 123.8 %attention_backward.1 = (bf16[128,4096]{1,0:T(8,128)(2,1)}, bf16[128,512]{1,0:T(8,128)(2,1)}, f32[16,512]{1,0:T(8,128)}) custom-call(s32[1,8]{1,0:T(1,128)} %length_ref.1, s32[32,32]{1,0:T(8,128)} %bitcast.16, bf16[16,512]{1,0:T(8,128)(2,1)} %weight_ref.1, bf16[128,4096]{1,0:T(8,128)(2,1)} %bitcast.9, bf16[128,512]{1,0:T(8,128)(2,1)} %bitcast.14, ...), custom_call_target="tpu_custom_call" | custom-call | tf_op jit(solution)/shard_map/attention_backward/pallas_call | solution.py:645
  124.4 0.0 copy-start
  124.4 2.3 %copy.15 = bf16[1,128,4096]{2,1,0:T(8,128)(2,1)} copy(bf16[1,128,4096]{2,1,0:T(8,128)(2,1)} %bitcast.13) | data formatting | bytes 2097152
  126.8 0.0 copy-done
  126.8 0.0 copy-start.1
  126.8 0.7 copy.16
  127.4 0.1 copy-done.1
  127.5 0.6 copy.17
Async XLA Ops:
  124.4 2.3 %copy-start = (bf16[128,512]{1,0:T(8,128)(2,1)S(1)}, bf16[128,512]{1,0:T(8,128)(2,1)}, u32[]{:S(2)}) copy-start(bf16[128,512]{1,0:T(8,128)(2,1)} %get-tuple-element.7) | copy-start | bytes 393220
  126.8 0.8 copy-start.1

commit v5 on v4

--- a/solution.py
+++ b/solution.py
@@ -387,6 +387,7 @@
     query_move.arrive()
     forward(0)
     ring(2)
+    saved_move.start()
     load_hidden.wait()
     forward(1)
     forward(2)
@@ -405,10 +406,23 @@
         value_part(quarter)
     value_rounded[...] = value_terms[...].astype(BF)
     value_back.start()
-    saved_move.start()
     for block in range(D // CHUNK):
         rows = slice(block * CHUNK, (block + 1) * CHUNK)
         turned[rows] = nt_dot(diagonal, hidden_ref[:, rows]).astype(BF)
+
+    saved_move.arrive()
+    saved_turned = nt_dot(diagonal, saved[...]).astype(BF)
+
+    @pl.loop(0, TOKENS // CHUNK)
+    def _(block):
+        rows = rows_at(block * CHUNK, CHUNK)
+        product = jnp.dot(
+            saved_turned, to_owner[:, rows], preferred_element_type=F32
+        ) * nt_dot(diagonal, grads[rows])
+        for head in range(2):
+            delta[head : head + 1, rows] = jnp.sum(
+                product[head * HD : (head + 1) * HD], axis=0, keepdims=True
+            )
 
     def four(arrived, group):
         total = arrived[4 * group].astype(F32)
@@ -495,31 +509,17 @@
                 ).astype(BF)
                 ring(step, part).start()
 
-    saved_move.arrive()
-    saved_turned = nt_dot(diagonal, saved[...]).astype(BF)
-
-    @pl.loop(0, TOKENS // CHUNK)
-    def _(block):
-        rows = rows_at(block * CHUNK, CHUNK)
-        product = jnp.dot(
-            saved_turned, to_owner[:, rows], preferred_element_type=F32
-        ) * nt_dot(diagonal, grads[rows])
-        for head in range(2):
-            delta[head : head + 1, rows] = jnp.sum(
-                product[head * HD : (head + 1) * HD], axis=0, keepdims=True
-            )
-
-    ring_back(1)
     value_move.arrive()
     backward(0)
     backward(1)
-    ring_back(2)
+    ring_back(1)
     backward(2)
     backward(3)
     key_rounded[...] = key_terms[...].astype(BF)
     key_back.start()
+    ring_back(2)
+    own_rows()
     ring_back(3)
-    own_rows()
     pair_back(7).wait_recv()
     for part in (0, 1):
         up_back(3, part).wait_recv()
@@ -650,7 +650,7 @@
             jax.ShapeDtypeStruct((CAP, KVW), F32),
         ),
         in_specs=[smem, smem, hbm, hbm, hbm, hbm, vmem, hbm, hbm],
-        out_specs=(vmem, vmem, vmem),
+        out_specs=(hbm, vmem, vmem),
         scratch_shapes=[
             pltpu.VMEM((ROWS, D), BF),
             pltpu.VMEM((D, ROWS), BF),

time: 130 us -> 121 us (0.931)
  Pallas kernels: 124 us -> 115 us
    pallas_call x1, Pallas kernels: 124 us -> 115 us  [local(): pl.pallas_call(kernel, out_shape=(jax.ShapeDtypeStruct((ROWS, D), BF), ja...]
where the time goes in v5:
time: 121 us; the launch traced here: 120 us
  Pallas kernels  115 us (95%)
  local copies, waits for them, and re-layouts  3.7 us (3%)
    pallas_call x1, Pallas kernels, local(): pl.pallas_call(kernel, out_shape=(jax.ShapeDtypeStruct((ROWS, D), BF), ja...  115 us
    unnamed x7, local copies, waits for them, and re-layouts  3.7 us

profile of v5, /device:TPU:1, one launch (start us, length us, event | category | flops | bytes accessed | tf_op | source)
XLA Modules:
  0.0 119.8 jit_solution(16231155902917852999)
XLA Ops:
  0.6 115.4 %attention_backward.1 = (bf16[128,4096]{1,0:T(8,128)(2,1)}, bf16[128,512]{1,0:T(8,128)(2,1)}, f32[16,512]{1,0:T(8,128)}) custom-call(s32[1,8]{1,0:T(1,128)} %length_ref.1, s32[32,32]{1,0:T(8,128)} %bitcast.16, bf16[16,512]{1,0:T(8,128)(2,1)} %weight_ref.1, bf16[128,4096]{1,0:T(8,128)(2,1)} %bitcast.9, bf16[128,512]{1,0:T(8,128)(2,1)} %bitcast.14, ...), custom_call_target="tpu_custom_call" | custom-call | tf_op jit(solution)/shard_map/attention_backward/pallas_call | solution.py:645
  116.1 0.0 copy-start
  116.1 2.3 %copy.15 = bf16[1,128,4096]{2,1,0:T(8,128)(2,1)} copy(bf16[1,128,4096]{2,1,0:T(8,128)(2,1)} %bitcast.13) | data formatting | bytes 2097152
  118.4 0.0 copy-done
  118.4 0.0 copy-start.1
  118.4 0.7 copy.16
  119.1 0.1 copy-done.1
  119.2 0.6 copy.17
Async XLA Ops:
  116.1 2.3 %copy-start = (bf16[128,512]{1,0:T(8,128)(2,1)S(1)}, bf16[128,512]{1,0:T(8,128)(2,1)}, u32[]{:S(2)}) copy-start(bf16[128,512]{1,0:T(8,128)(2,1)} %get-tuple-element.7) | copy-start | bytes 393220
  118.4 0.8 copy-start.1

commit v6 on v5

--- a/solution.py
+++ b/solution.py
@@ -92,6 +92,71 @@
         @pl.loop(1, CTX)
         def _(step):
             self.copy(step).wait_send()
+
+
+class Shared:
+    def __init__(self, source, target, sems, near_sems, own_sem, dp, ctx):
+        self.source, self.target = source, target
+        self.sems, self.near_sems, self.own_sem = sems, near_sems, own_sem
+        self.dp, self.ctx = dp, ctx
+        self.chip, self.core = ctx // 2, ctx % 2
+
+    def block(self, device):
+        return self.target.at[rows_at(device * ROWS, ROWS)]
+
+    def far(self, step):
+        partner = ((self.chip + step) % 8) * 2 + self.core
+        return remote(
+            self.source(partner),
+            self.block(self.ctx),
+            self.sems.at[0, step],
+            self.sems.at[1, step],
+            self.dp,
+            partner,
+        )
+
+    def near(self, step, core):
+        block = self.block(((self.chip + 8 - step) % 8) * 2 + core)
+        return remote(
+            block,
+            block,
+            self.near_sems.at[0, step],
+            self.near_sems.at[1, step],
+            self.dp,
+            self.ctx + 1 - 2 * self.core,
+        )
+
+    def own_copy(self):
+        return pltpu.make_async_copy(self.source(self.ctx), self.block(self.ctx), self.own_sem)
+
+    def start(self):
+        self.own_copy().start()
+
+        @pl.loop(1, 8)
+        def _(step):
+            self.far(step).start()
+
+    def hand_on(self):
+        self.own_copy().wait()
+        self.near(0, self.core).start()
+
+        @pl.loop(1, 8)
+        def _(step):
+            self.far(step).wait_recv()
+            self.near(step, self.core).start()
+
+    def arrive(self):
+        @pl.loop(0, 8)
+        def _(step):
+            self.near(step, 1 - self.core).wait_recv()
+
+    def finish(self):
+        self.near(0, self.core).wait_send()
+
+        @pl.loop(1, 8)
+        def _(step):
+            self.far(step).wait_send()
+            self.near(step, self.core).wait_send()
 
 
 def plane_partner(dp, ctx, step):
@@ -149,6 +214,7 @@
     ring_sems,
     pair_sems,
     exchange_sems,
+    shared_sems,
     pair_back_sems,
     ring_back_sems,
     plane_back_sems,
@@ -227,11 +293,17 @@
     def exchange(which, source, target):
         return Exchange(source, target, exchange_sems.at[which], own_sems.at[4 + which], dp, ctx)
 
-    key_move = exchange(0, lambda to: key_hbm.at[:, wide(to // 4, HD)], keys.at[here])
+    def shared(which, source, target):
+        near_sems = shared_sems.at[which // 4]
+        return Shared(
+            source, target, exchange_sems.at[which], near_sems, own_sems.at[4 + which], dp, ctx
+        )
+
+    key_move = shared(0, lambda to: key_hbm.at[:, wide(to // 4, HD)], keys)
     query_move = exchange(1, lambda to: query_hbm.at[:, wide(to, PAIR)], queries.at[here])
     grad_move = exchange(2, lambda to: grad_hbm.at[:, wide(to, PAIR)], grads.at[here])
     saved_move = exchange(3, lambda to: saved_hbm.at[:, wide(to, PAIR)], saved.at[here])
-    value_move = exchange(4, lambda to: value_own.at[:, wide(to // 4, HD)], values.at[here])
+    value_move = shared(4, lambda to: value_own.at[:, wide(to // 4, HD)], values)
     value_back = exchange(5, lambda to: value_rounded.at[rows_at(to * ROWS, ROWS)], value_in.at[ctx])
     key_back = exchange(6, lambda to: key_rounded.at[rows_at(to * ROWS, ROWS)], key_in.at[ctx])
     query_back = exchange(
@@ -303,7 +375,7 @@
         rows = rows_at(block * ROWS, ROWS)
         return jnp.concatenate([pairs[rows, :HD], pairs[rows, HD:]], axis=0)
 
-    def forward(quarter):
+    def forward(quarter, behind=()):
         first, size = quarters[quarter]
 
         @pl.loop(first, first + 4)
@@ -330,20 +402,26 @@
             scores = nt_dot(keys[window], stacked(queries, block))
             scores = scores + jnp.concatenate([bias[:size], bias[:size]], axis=1)
             top = jnp.max(scores, axis=0, keepdims=True)
-            raised = jnp.exp((scores - top) * SCALE)
+            raised = jnp.exp2((scores - top) * (SCALE * math.log2(math.e)))
             weights = raised * (1.0 / jnp.sum(raised, axis=0, keepdims=True))
             weights_all[pl.ds(pl.multiple_of(block * USED, ROWS), size)] = weights.astype(BF)
+            for earlier in behind:
+                value_block(earlier, block - first + quarters[earlier][0])
+
+    def value_block(quarter, block):
+        size = quarters[quarter][1]
+        window = pl.ds(pl.multiple_of(first_block(quarter, block) * ROWS, ROWS), size)
+        stored = pl.ds(pl.multiple_of(block * USED, ROWS), size)
+        value_terms[window] += jnp.dot(
+            weights_all[stored], stacked(grads, block), preferred_element_type=F32
+        )
 
     def value_part(quarter):
-        first, size = quarters[quarter]
+        first = quarters[quarter][0]
 
         @pl.loop(first, first + 4)
         def _(block):
-            window = pl.ds(pl.multiple_of(first_block(quarter, block) * ROWS, ROWS), size)
-            stored = pl.ds(pl.multiple_of(block * USED, ROWS), size)
-            value_terms[window] += jnp.dot(
-                weights_all[stored], stacked(grads, block), preferred_element_type=F32
-            )
+            value_block(quarter, block)
 
     def backward(quarter):
         first, size = quarters[quarter]
@@ -356,15 +434,14 @@
             weights = weights_all[stored].astype(F32)
             dweights = nt_dot(values[window], stacked(grads, block))
             row_delta = jnp.concatenate([delta[:1, rows], delta[1:, rows]], axis=1)
-            dscores = (
-                (weights * SCALE) * (dweights.astype(BF).astype(F32) - row_delta)
-            ).astype(BF)
+            dscores = (weights * (dweights - row_delta)).astype(BF)
             key_terms[window] += jnp.dot(
                 dscores, stacked(queries, block), preferred_element_type=F32
             )
             query_turned = jnp.dot(
                 keys_turned[:, window], dscores, preferred_element_type=F32
-            ).astype(BF)
+            )
+            query_turned = (query_turned * SCALE).astype(BF)
             for head in range(2):
                 columns = slice(head * HD, (head + 1) * HD)
                 query_rows[rows, columns] = nt_dot(same, query_turned[:, columns]).astype(BF)
@@ -379,9 +456,10 @@
 
         query_back.start()
 
+    key_move.hand_on()
+    ring(0)
     key_move.arrive()
     keys_turned[...] = nt_dot(same, keys[...]).astype(BF)
-    ring(0)
     ring(1)
     grad_move.start()
     query_move.arrive()
@@ -400,10 +478,9 @@
             pair(1 - core, offset, part).wait_recv()
     value_own[...] = jnp.dot(hidden_ref[...], whole[...], preferred_element_type=F32).astype(BF)
     value_move.start()
-    forward(3)
     grad_move.arrive()
-    for quarter in range(4):
-        value_part(quarter)
+    forward(3, (0, 1, 2))
+    value_part(3)
     value_rounded[...] = value_terms[...].astype(BF)
     value_back.start()
     for block in range(D // CHUNK):
@@ -423,6 +500,8 @@
             delta[head : head + 1, rows] = jnp.sum(
                 product[head * HD : (head + 1) * HD], axis=0, keepdims=True
             )
+
+    value_move.hand_on()
 
     def four(arrived, group):
         total = arrived[4 * group].astype(F32)
@@ -515,7 +594,7 @@
     ring_back(1)
     backward(2)
     backward(3)
-    key_rounded[...] = key_terms[...].astype(BF)
+    key_rounded[...] = (key_terms[...] * SCALE).astype(BF)
     key_back.start()
     ring_back(2)
     own_rows()
@@ -689,6 +768,7 @@
             dma((4, 4, 2)),
             dma((2, 8, 2)),
             dma((8, 2, CTX)),
+            dma((2, 2, 8)),
             dma((2, 8)),
             dma((4, 4, 2)),
             dma((2, 16)),

time: 121 us -> 119 us (0.983)
  the two profiles are of different devices: /device:TPU:1 before, /device:TPU:5 now
where the time goes in v6:
time: 119 us
  Pallas kernels  114 us (96%)
  local copies, waits for them, and re-layouts  3.7 us (3%)
    pallas_call x1, Pallas kernels, local(): pl.pallas_call(kernel, out_shape=(jax.ShapeDtypeStruct((ROWS, D), BF), ja...  114 us
    unnamed x7, local copies, waits for them, and re-layouts  3.7 us

profile of v6, /device:TPU:5, one launch (start us, length us, event | category | flops | bytes accessed | tf_op | source)
XLA Modules:
  0.0 118.7 jit_solution(2149016197035922886)
XLA Ops:
  0.6 114.3 %attention_backward.1 = (bf16[128,4096]{1,0:T(8,128)(2,1)}, bf16[128,512]{1,0:T(8,128)(2,1)}, f32[16,512]{1,0:T(8,128)}) custom-call(s32[1,8]{1,0:T(1,128)} %length_ref.1, s32[32,32]{1,0:T(8,128)} %bitcast.16, bf16[16,512]{1,0:T(8,128)(2,1)} %weight_ref.1, bf16[128,4096]{1,0:T(8,128)(2,1)} %bitcast.9, bf16[128,512]{1,0:T(8,128)(2,1)} %bitcast.14, ...), custom_call_target="tpu_custom_call" | custom-call | tf_op jit(solution)/shard_map/attention_backward/pallas_call | solution.py:724
  115.0 0.0 copy-start
  115.0 2.3 %copy.15 = bf16[1,128,4096]{2,1,0:T(8,128)(2,1)} copy(bf16[1,128,4096]{2,1,0:T(8,128)(2,1)} %bitcast.13) | data formatting | bytes 2097152
  117.3 0.0 copy-done
  117.3 0.0 copy-start.1
  117.3 0.7 copy.16
  118.0 0.1 copy-done.1
  118.1 0.6 copy.17
Async XLA Ops:
  115.0 2.3 %copy-start = (bf16[128,512]{1,0:T(8,128)(2,1)S(1)}, bf16[128,512]{1,0:T(8,128)(2,1)}, u32[]{:S(2)}) copy-start(bf16[128,512]{1,0:T(8,128)(2,1)} %get-tuple-element.7) | copy-start | bytes 393220
  117.3 0.8 copy-start.1

commit v7 on v6

--- a/solution.py
+++ b/solution.py
@@ -273,18 +273,6 @@
 
     own_shard = pltpu.make_async_copy(weight_ref, shard, own_sems.at[3])
 
-    @pl.when(core == x_lo)
-    def _():
-        own_shard.start()
-
-    @pl.when(core != x_lo)
-    def _():
-        plane_copy(0).start()
-
-    @pl.loop(1, 16)
-    def _(step):
-        plane_copy(step).start()
-
     def wide(index, width):
         return pl.ds(pl.multiple_of(index * width, width), width)
 
@@ -310,6 +298,18 @@
         7, lambda to: query_owned.at[rows_at(to * ROWS, ROWS)], query_grad_ref.at[:, wide(ctx, PAIR)]
     )
     key_move.start()
+    @pl.when(core == x_lo)
+    def _():
+        own_shard.start()
+
+    @pl.when(core != x_lo)
+    def _():
+        plane_copy(0).start()
+
+    @pl.loop(1, 16)
+    def _(step):
+        plane_copy(step).start()
+
     query_move.start()
 
     @pl.when(core == x_lo)

time: 119 us -> 120 us (level)
  the two profiles are of different devices: /device:TPU:5 before, /device:TPU:69 now
where the time goes in v7:
time: 120 us; the launch traced here: 119 us
  Pallas kernels  115 us (96%)
  local copies, waits for them, and re-layouts  3.7 us (3%)
    pallas_call x1, Pallas kernels, local(): pl.pallas_call(kernel, out_shape=(jax.ShapeDtypeStruct((ROWS, D), BF), ja...  115 us
    unnamed x7, local copies, waits for them, and re-layouts  3.7 us

profile of v7, /device:TPU:69, one launch (start us, length us, event | category | flops | bytes accessed | tf_op | source)
XLA Modules:
  0.0 119.5 jit_solution(11992179594808302531)
XLA Ops:
  0.6 115.1 %attention_backward.1 = (bf16[128,4096]{1,0:T(8,128)(2,1)}, bf16[128,512]{1,0:T(8,128)(2,1)}, f32[16,512]{1,0:T(8,128)}) custom-call(s32[1,8]{1,0:T(1,128)} %length_ref.1, s32[32,32]{1,0:T(8,128)} %bitcast.16, bf16[16,512]{1,0:T(8,128)(2,1)} %weight_ref.1, bf16[128,4096]{1,0:T(8,128)(2,1)} %bitcast.9, bf16[128,512]{1,0:T(8,128)(2,1)} %bitcast.14, ...), custom_call_target="tpu_custom_call" | custom-call | tf_op jit(solution)/shard_map/attention_backward/pallas_call | solution.py:724
  115.8 0.0 copy-start
  115.8 2.3 %copy.15 = bf16[1,128,4096]{2,1,0:T(8,128)(2,1)} copy(bf16[1,128,4096]{2,1,0:T(8,128)(2,1)} %bitcast.13) | data formatting | bytes 2097152
  118.1 0.0 copy-done
  118.1 0.0 copy-start.1
  118.1 0.7 copy.16
  118.8 0.1 copy-done.1
  118.9 0.6 copy.17
Async XLA Ops:
  115.8 2.3 %copy-start = (bf16[128,512]{1,0:T(8,128)(2,1)S(1)}, bf16[128,512]{1,0:T(8,128)(2,1)}, u32[]{:S(2)}) copy-start(bf16[128,512]{1,0:T(8,128)(2,1)} %get-tuple-element.7) | copy-start | bytes 393220
  118.1 0.8 copy-start.1
